TPU v7x, 32 devices: a whole 2x2x4 slice. The times are simulated.
32 devices in a mesh: dp: 4 (over y, x), seq: 8 (over z, core).
Axes of the slice: x: 2, y: 2, z: 4, core: 2. Of those that a mesh axis runs over, the one named last changes fastest.
Arguments:
- tokens: bfloat16 [2, 4096, 1088], P(None, ('dp', 'seq')), may hold values from -6 to 6
- cotangent: bfloat16 [2, 4096, 1088], P(None, ('dp', 'seq')), may hold values from -6 to 6
- w_qkv: bfloat16 [1088, 3264], P('dp', 'seq'), may hold values from -0.1875 to 0.1875
- w_out: bfloat16 [1088, 1088], P('dp', 'seq'), may hold values from -1.5 to 1.5
- w_up: bfloat16 [1088, 4352], P('dp', 'seq'), may hold values from -0.1875 to 0.1875
- w_down: bfloat16 [4352, 1088], P('dp', 'seq'), may hold values from -0.09375 to 0.09375
- gain_one: bfloat16 [1088], P('dp'), may hold values from 0.25 to 1.75
- bias_one: bfloat16 [1088], P('dp'), may hold values from -3 to 3
- gain_two: bfloat16 [1088], P('dp'), may hold values from 0.25 to 1.75
- bias_two: bfloat16 [1088], P('dp'), may hold values from -3 to 3
- lengths: int32 [2, 4, 8], P(None, 'dp'), may hold values from 1 to 896, 1024 in all within a row
- slot_order: int32 [2, 4, 8], P(None, 'dp'), may hold values from 0 to 7, each once within a row
Outputs:
- block_out: bfloat16 [2, 4096, 1088], P(None, ('dp', 'seq'))
- grad_input: bfloat16 [2, 4096, 1088], P(None, ('dp', 'seq'))
- grad_qkv: float32 [1088, 3264], P('dp', 'seq')
- grad_proj: float32 [1088, 1088], P('dp', 'seq')
- grad_up: float32 [1088, 4352], P('dp', 'seq')
- grad_down: float32 [4352, 1088], P('dp', 'seq')
- grad_gain_one: float32 [1088], P('dp')
- grad_bias_one: float32 [1088], P('dp')
- grad_gain_two: float32 [1088], P('dp')
- grad_bias_two: float32 [1088], P('dp')
Inputs may be any that keep to these rules, and one draw needn't show every extreme that they name: For each micro-batch and group the 8 lengths sum to 1024; the largest is exactly 896. `slot_order`: each row over the last dimension holds every number below 8 once.
All inputs are finite; a program needn't handle non-finite values.
Results may differ from a plain program's by a relative error of at most 0.02.
Values may be sent and summed in bfloat16 or wider, within the bound.
A program may use at most 192 MiB of HBM per device.

v0:
```python
import jax
import jax.numpy as jnp
from jax import lax
from jax.sharding import PartitionSpec as P

HEADS = 17


EPS = 1e-05
NEG = -1e30
GELU_C = 0.7978845608028654
block_rows = 512


def from_behind(block, axis, distance):
    devices = range(lax.axis_size(axis))
    route = [((i - distance) % len(devices), i) for i in devices]
    return lax.ppermute(block, axis, route)


def gelu_tanh(values):
    return 0.5 * values * (1.0 + jnp.tanh(GELU_C * (values + 0.044715 * values * values * values)))


def normalize(residual):
    row_mean = jnp.mean(residual, -1, keepdims=True)
    centered = residual - row_mean
    inv_std = lax.rsqrt(jnp.mean(centered * centered, -1, keepdims=True) + EPS)
    return (centered * inv_std, inv_std)


def norm_back(grad_normed, scaled, inv_std, gain_row):
    grad_scaled = grad_normed * gain_row
    return inv_std * (
        grad_scaled
        - jnp.mean(grad_scaled, -1, keepdims=True)
        - scaled * jnp.mean(grad_scaled * scaled, -1, keepdims=True)
    )


def segment_of(places, doc_ends):
    return jnp.sum((places[:, None] >= doc_ends[None, :]).astype(jnp.int32), 1)


def key_places(first_row, key_count, slot_row, doc_ends, tok_dev):
    row_index = first_row + jnp.arange(key_count, dtype=jnp.int32)
    source_slot = row_index // tok_dev
    slot_ids = jnp.arange(slot_row.shape[0], dtype=jnp.int32)
    base_slot = jnp.sum(
        jnp.where(source_slot[:, None] == slot_ids[None, :], slot_row[None, :], 0), 1
    )
    places = base_slot * tok_dev + row_index % tok_dev
    return (places, segment_of(places, doc_ends))


def masked_scores(queries, key_block, q_place, q_segment, k_place, k_segment, score_scale):
    key_heads = key_block.reshape(key_block.shape[0], queries.shape[1], queries.shape[2])
    scores = (
        jnp.einsum("qhd,khd->hqk", queries, key_heads, preferred_element_type=jnp.float32)
        * score_scale
    )
    allowed = (q_segment[:, None] == k_segment[None, :]) & (k_place[None, :] <= q_place[:, None])
    return (jnp.where(allowed[None], scores, -jnp.inf), key_heads)


def fold_keys(state_now, key_block, value_block, first_row, context):
    queries, q_place, q_segment, slot_row, doc_ends, score_scale = context
    running_max, running_sum, accum_out = state_now
    k_place, k_segment = key_places(
        first_row, key_block.shape[0], slot_row, doc_ends, queries.shape[0]
    )
    scores, key_heads = masked_scores(
        queries, key_block, q_place, q_segment, k_place, k_segment, score_scale
    )
    value_heads = value_block.reshape(key_heads.shape)
    new_max = jnp.maximum(running_max, jnp.max(scores, -1))
    weights = jnp.exp(scores - new_max[..., None])
    factor = jnp.exp(running_max - new_max)
    running_sum = running_sum * factor + jnp.sum(weights, -1)
    accum_out = accum_out * factor.T[:, :, None] + jnp.einsum(
        "hqk,khd->qhd",
        weights.astype(jnp.bfloat16),
        value_heads,
        preferred_element_type=jnp.float32,
    )
    return (new_max, running_sum, accum_out)


def back_block(
    queries,
    grad_heads,
    key_block,
    value_block,
    q_place,
    q_segment,
    k_place,
    k_segment,
    log_sum,
    row_dot,
    score_scale,
):
    scores, key_heads = masked_scores(
        queries, key_block, q_place, q_segment, k_place, k_segment, score_scale
    )
    value_heads = value_block.reshape(key_heads.shape)
    probabilities = jnp.exp(scores - log_sum[..., None])
    grad_probs = jnp.einsum(
        "qhd,khd->hqk", grad_heads, value_heads, preferred_element_type=jnp.float32
    )
    grad_scores = (probabilities * (grad_probs - row_dot[..., None])).astype(jnp.bfloat16)
    grad_query = score_scale * jnp.einsum(
        "hqk,khd->qhd", grad_scores, key_heads, preferred_element_type=jnp.float32
    )
    grad_keys = score_scale * jnp.einsum(
        "hqk,qhd->khd", grad_scores, queries, preferred_element_type=jnp.float32
    )
    grad_values = jnp.einsum(
        "hqk,qhd->khd",
        probabilities.astype(jnp.bfloat16),
        grad_heads,
        preferred_element_type=jnp.float32,
    )
    return (grad_query, grad_keys.reshape(key_block.shape), grad_values.reshape(key_block.shape))


def shards(
    tokens,
    cotangent,
    w_qkv,
    w_out,
    w_up,
    w_down,
    gain_one,
    bias_one,
    gain_two,
    bias_two,
    lengths,
    slot_order,
):
    micro_count, tok_dev, width = tokens.shape
    head_dim = width // HEADS
    score_scale = head_dim ** (-0.5)
    n_seq = lax.axis_size("seq")
    my_slot = lax.axis_index("seq")
    slot_ids = jnp.arange(n_seq, dtype=jnp.int32)
    ffn_width = w_up.shape[1] * n_seq
    sum_qkv = jnp.zeros((width, 3 * width), jnp.float32)
    sum_out = jnp.zeros((width, width), jnp.float32)
    sum_up = jnp.zeros((width, ffn_width), jnp.float32)
    sum_down = jnp.zeros((ffn_width, width), jnp.float32)
    sum_gain_one = jnp.zeros((width,), jnp.float32)
    sum_bias_one = jnp.zeros((width,), jnp.float32)
    sum_gain_two = jnp.zeros((width,), jnp.float32)
    sum_bias_two = jnp.zeros((width,), jnp.float32)
    out_rows = []
    input_grads = []
    for micro_index in range(micro_count):
        col_parts = (
            lax.all_gather(w_qkv, "seq", axis=1, tiled=True),
            lax.all_gather(w_out, "seq", axis=1, tiled=True),
            lax.all_gather(w_up, "seq", axis=1, tiled=True),
            lax.all_gather(w_down, "seq", axis=1, tiled=True),
        )
        full_qkv, full_out, full_up, full_down, g_one, b_one, g_two, b_two = (
            lax.all_gather(col_parts[0], "dp", axis=0, tiled=True),
            lax.all_gather(col_parts[1], "dp", axis=0, tiled=True),
            lax.all_gather(col_parts[2], "dp", axis=0, tiled=True),
            lax.all_gather(col_parts[3], "dp", axis=0, tiled=True),
            lax.all_gather(gain_one, "dp", axis=0, tiled=True),
            lax.all_gather(bias_one, "dp", axis=0, tiled=True),
            lax.all_gather(gain_two, "dp", axis=0, tiled=True),
            lax.all_gather(bias_two, "dp", axis=0, tiled=True),
        )
        slot_row = slot_order[micro_index, 0]
        doc_ends = jnp.cumsum(lengths[micro_index, 0])
        base_slot = jnp.sum(jnp.where(slot_ids == my_slot, slot_row, 0))
        q_place = base_slot * tok_dev + jnp.arange(tok_dev, dtype=jnp.int32)
        q_segment = segment_of(q_place, doc_ends)
        residual = tokens[micro_index].astype(jnp.float32)
        scaled_one, inv_one = normalize(residual)
        normed_one = (scaled_one * g_one.astype(jnp.float32) + b_one.astype(jnp.float32)).astype(
            jnp.bfloat16
        )
        qkv_all = jnp.dot(normed_one, full_qkv, preferred_element_type=jnp.float32).astype(
            jnp.bfloat16
        )
        queries = qkv_all[:, :width].reshape(tok_dev, HEADS, head_dim)
        key_local = qkv_all[:, width : 2 * width]
        value_local = qkv_all[:, 2 * width :]
        context = (queries, q_place, q_segment, slot_row, doc_ends, score_scale)

        def attend(state_now, key_piece, first_row, context=context):
            key_part, value_part = key_piece
            key_count = key_part.shape[0]
            blocks = key_count // block_rows

            def scan_step(inner_state, block_item):
                return (
                    fold_keys(
                        inner_state,
                        block_item[0],
                        block_item[1],
                        block_item[2] * block_rows,
                        context,
                    ),
                    None,
                )

            final_state, _ = lax.scan(
                scan_step,
                state_now,
                (
                    key_part.reshape(blocks, block_rows, width),
                    value_part.reshape(blocks, block_rows, width),
                    jnp.arange(blocks, dtype=jnp.int32),
                ),
            )
            return final_state

        start_state = (
            jnp.full((HEADS, tok_dev), NEG, jnp.float32),
            jnp.zeros((HEADS, tok_dev), jnp.float32),
            jnp.zeros((tok_dev, HEADS, head_dim), jnp.float32),
        )
        running_max, running_sum, accum_out = attend(
            start_state,
            (
                lax.all_gather(key_local, "seq", axis=0, tiled=True),
                lax.all_gather(value_local, "seq", axis=0, tiled=True),
            ),
            jnp.int32(0),
        )
        attended = accum_out / running_sum.T[:, :, None]
        log_sum = running_max + jnp.log(running_sum)
        attn_flat = attended.reshape(tok_dev, width).astype(jnp.bfloat16)
        middle = residual + jnp.dot(attn_flat, full_out, preferred_element_type=jnp.float32)
        scaled_two, inv_two = normalize(middle)
        normed_two = (scaled_two * g_two.astype(jnp.float32) + b_two.astype(jnp.float32)).astype(
            jnp.bfloat16
        )
        hidden = jnp.dot(normed_two, full_up, preferred_element_type=jnp.float32)
        activated_full, gelu_back = jax.vjp(gelu_tanh, hidden)
        activated = activated_full.astype(jnp.bfloat16)
        block_out = middle + jnp.dot(activated, full_down, preferred_element_type=jnp.float32)
        out_rows.append(block_out.astype(jnp.bfloat16))
        back_parts = (
            lax.all_gather(w_qkv, "seq", axis=1, tiled=True),
            lax.all_gather(w_out, "seq", axis=1, tiled=True),
            lax.all_gather(w_up, "seq", axis=1, tiled=True),
            lax.all_gather(w_down, "seq", axis=1, tiled=True),
        )
        back_qkv, back_out, back_up, back_down, back_gain_one, back_gain_two = (
            lax.all_gather(back_parts[0], "dp", axis=0, tiled=True),
            lax.all_gather(back_parts[1], "dp", axis=0, tiled=True),
            lax.all_gather(back_parts[2], "dp", axis=0, tiled=True),
            lax.all_gather(back_parts[3], "dp", axis=0, tiled=True),
            lax.all_gather(gain_one, "dp", axis=0, tiled=True),
            lax.all_gather(gain_two, "dp", axis=0, tiled=True),
        )
        grad_rows = cotangent[micro_index]
        sum_down = sum_down + jnp.einsum(
            "tf,td->fd", activated, grad_rows, preferred_element_type=jnp.float32
        )
        grad_act = jnp.einsum("td,fd->tf", grad_rows, back_down, preferred_element_type=jnp.float32)
        grad_hidden = gelu_back(grad_act)[0].astype(jnp.bfloat16)
        sum_up = sum_up + jnp.einsum(
            "td,tf->df", normed_two, grad_hidden, preferred_element_type=jnp.float32
        )
        grad_normed_two = jnp.einsum(
            "tf,df->td", grad_hidden, back_up, preferred_element_type=jnp.float32
        )
        sum_gain_two = sum_gain_two + jnp.sum(grad_normed_two * scaled_two, 0)
        sum_bias_two = sum_bias_two + jnp.sum(grad_normed_two, 0)
        grad_middle = grad_rows.astype(jnp.float32) + norm_back(
            grad_normed_two, scaled_two, inv_two, back_gain_two.astype(jnp.float32)
        )
        grad_branch = grad_middle.astype(jnp.bfloat16)
        sum_out = sum_out + jnp.einsum(
            "td,te->de", attn_flat, grad_branch, preferred_element_type=jnp.float32
        )
        grad_attn = jnp.einsum(
            "te,de->td", grad_branch, back_out, preferred_element_type=jnp.float32
        ).astype(jnp.bfloat16)
        grad_heads = grad_attn.reshape(tok_dev, HEADS, head_dim)
        row_dot = jnp.einsum("qhd,qhd->hq", grad_heads.astype(jnp.float32), attended)
        stacked = jnp.stack(
            [
                key_local.astype(jnp.float32),
                value_local.astype(jnp.float32),
                jnp.zeros((tok_dev, width), jnp.float32),
                jnp.zeros((tok_dev, width), jnp.float32),
            ]
        )

        def return_step(
            step_index,
            loop_state,
            queries=queries,
            grad_heads=grad_heads,
            q_place=q_place,
            q_segment=q_segment,
            slot_row=slot_row,
            doc_ends=doc_ends,
            log_sum=log_sum,
            row_dot=row_dot,
        ):
            carried, grad_query = loop_state
            source = (my_slot - step_index) % n_seq
            k_place, k_segment = key_places(source * tok_dev, tok_dev, slot_row, doc_ends, tok_dev)
            part_query, part_keys, part_values = back_block(
                queries,
                grad_heads,
                carried[0].astype(jnp.bfloat16),
                carried[1].astype(jnp.bfloat16),
                q_place,
                q_segment,
                k_place,
                k_segment,
                log_sum,
                row_dot,
                score_scale,
            )
            carried = jnp.stack(
                [carried[0], carried[1], carried[2] + part_keys, carried[3] + part_values]
            )
            carried = from_behind(carried.astype(jnp.bfloat16), "seq", 1).astype(carried.dtype)
            return (carried, grad_query + part_query)

        stacked, grad_query = lax.fori_loop(
            0, n_seq, return_step, (stacked, jnp.zeros((tok_dev, HEADS, head_dim), jnp.float32))
        )
        key_grad, value_grad = (stacked[2], stacked[3])
        grad_qkv_rows = jnp.concatenate(
            [grad_query.reshape(tok_dev, width), key_grad, value_grad], 1
        ).astype(jnp.bfloat16)
        sum_qkv = sum_qkv + jnp.einsum(
            "td,te->de", normed_one, grad_qkv_rows, preferred_element_type=jnp.float32
        )
        grad_normed_one = jnp.einsum(
            "te,de->td", grad_qkv_rows, back_qkv, preferred_element_type=jnp.float32
        )
        sum_gain_one = sum_gain_one + jnp.sum(grad_normed_one * scaled_one, 0)
        sum_bias_one = sum_bias_one + jnp.sum(grad_normed_one, 0)
        grad_input = grad_middle + norm_back(
            grad_normed_one, scaled_one, inv_one, back_gain_one.astype(jnp.float32)
        )
        input_grads.append(grad_input.astype(jnp.bfloat16))
    col_sums = (
        lax.psum_scatter(
            sum_qkv.astype(jnp.bfloat16), "seq", scatter_dimension=1, tiled=True
        ).astype(jnp.float32),
        lax.psum_scatter(
            sum_out.astype(jnp.bfloat16), "seq", scatter_dimension=1, tiled=True
        ).astype(jnp.float32),
        lax.psum_scatter(
            sum_up.astype(jnp.bfloat16), "seq", scatter_dimension=1, tiled=True
        ).astype(jnp.float32),
        lax.psum_scatter(
            sum_down.astype(jnp.bfloat16), "seq", scatter_dimension=1, tiled=True
        ).astype(jnp.float32),
    )
    reduced = (
        lax.psum_scatter(
            col_sums[0].astype(jnp.bfloat16), "dp", scatter_dimension=0, tiled=True
        ).astype(jnp.float32),
        lax.psum_scatter(
            col_sums[1].astype(jnp.bfloat16), "dp", scatter_dimension=0, tiled=True
        ).astype(jnp.float32),
        lax.psum_scatter(
            col_sums[2].astype(jnp.bfloat16), "dp", scatter_dimension=0, tiled=True
        ).astype(jnp.float32),
        lax.psum_scatter(
            col_sums[3].astype(jnp.bfloat16), "dp", scatter_dimension=0, tiled=True
        ).astype(jnp.float32),
        lax.psum_scatter(
            sum_gain_one.astype(jnp.bfloat16), "dp", scatter_dimension=0, tiled=True
        ).astype(jnp.float32),
        lax.psum_scatter(
            sum_bias_one.astype(jnp.bfloat16), "dp", scatter_dimension=0, tiled=True
        ).astype(jnp.float32),
        lax.psum_scatter(
            sum_gain_two.astype(jnp.bfloat16), "dp", scatter_dimension=0, tiled=True
        ).astype(jnp.float32),
        lax.psum_scatter(
            sum_bias_two.astype(jnp.bfloat16), "dp", scatter_dimension=0, tiled=True
        ).astype(jnp.float32),
    )
    norm_totals = lax.psum((reduced[4], reduced[5], reduced[6], reduced[7]), "seq")
    return (
        jnp.stack(out_rows),
        jnp.stack(input_grads),
        reduced[0],
        reduced[1],
        reduced[2],
        reduced[3],
        norm_totals[0],
        norm_totals[1],
        norm_totals[2],
        norm_totals[3],
    )


def solution(mesh):
    return jax.shard_map(
        shards,
        mesh=mesh,
        in_specs=(
            P(None, ("dp", "seq"), None),
            P(None, ("dp", "seq"), None),
            P("dp", "seq"),
            P("dp", "seq"),
            P("dp", "seq"),
            P("dp", "seq"),
            P("dp"),
            P("dp"),
            P("dp"),
            P("dp"),
            P(None, "dp", None),
            P(None, "dp", None),
        ),
        out_specs=(
            P(None, ("dp", "seq"), None),
            P(None, ("dp", "seq"), None),
            P("dp", "seq"),
            P("dp", "seq"),
            P("dp", "seq"),
            P("dp", "seq"),
            P("dp"),
            P("dp"),
            P("dp"),
            P("dp"),
        ),
        check_vma=False,
    )
```

profile of v0, /device:TPU:0, one launch (start us, length us, event | category | flops | bytes accessed | tf_op | source)
XLA Modules:
  0.0 1483.8 jit_solution(16310020791881566228)
XLA Ops:
  8.0 34.6 %all-gather.32.cloned.1.call-done = bf16[8,408,272]{1,2,0:T(8,128)(2,1)} async-done(((bf16[1,408,272]{1,2,0:T(8,128)(2,1)}), bf16[8,408,272]{1,2,0:T(8,128)(2,1)}) %all-gather.32.cloned.1.call-update) | async-done | bytes 1775632 | tf_op jit(solution)/shard_map/all_gather | solution.py:159
  53.4 16.2 %all-reduce.13 = (bf16[1088]{0:T(1024)(128)(2,1)S(1)}, bf16[1088]{0:T(1024)(128)(2,1)S(1)}, bf16[1088]{0:T(1024)(128)(2,1)S(1)}, bf16[1088]{0:T(1024)(128)(2,1)S(1)}) all-reduce(bf16[1088]{0:T(1024)(128)(2,1)S(1)} %dynamic-update-slice.1, bf16[1088]{0:T(1024)(128)(2,1)S(1)} %dynamic-update-slice, ...), channel_id=1, replica_groups=mesh['dp'=4,'seq'=8] {'dp'}, use_global_device_ids=true, to_apply=%add.1 | all-reduce | flops 4352 | bytes 17408
  70.0 57.6 %all-gather.14.cloned.1.call-done = bf16[1088,3264]{1,0:T(8,128)(2,1)} async-done(((bf16[272,3264]{1,0:T(8,128)(2,1)}), bf16[1088,3264]{1,0:T(8,128)(2,1)}) %all-gather.14.cloned.1.call-update) | async-done | bytes 7102480 | tf_op jit(solution)/shard_map/all_gather | solution.py:165
  144.8 21.1 %all_gather.38 = bf16[272,1088]{0,1:T(8,128)(2,1)S(1)} all-gather(bf16[272,136]{0,1:T(8,128)(2,1)S(1)} %copy-done.60), channel_id=1, replica_groups=mesh['dp'=4,'seq'=8] {'seq'}, dimensions={1}, use_global_device_ids=true | all-gather | bytes 665856 | tf_op jit(solution)/shard_map/all_gather | solution.py:160
  184.1 20.5 %all-gather.24.cloned.1.call-done = bf16[1088,1088]{0,1:T(8,128)(2,1)} async-done(((bf16[1088,136]{0,1:T(8,128)(2,1)}), bf16[1088,1088]{0,1:T(8,128)(2,1)}) %all-gather.24.cloned.1.call-update) | async-done | bytes 2367504 | tf_op jit(solution)/shard_map/all_gather | solution.py:162
  213.5 23.4 %all-gather.18.cloned.1.call-done = bf16[1024,1088]{0,1:T(8,128)(2,1)} async-done(((bf16[128,1088]{0,1:T(8,128)(2,1)}), bf16[1024,1088]{0,1:T(8,128)(2,1)}) %all-gather.18.cloned.1.call-update) | async-done | bytes 2228240 | tf_op jit(solution)/shard_map/all_gather | solution.py:229
  240.1 29.1 %all-gather.16.cloned.1.call-done = bf16[1024,1088]{0,1:T(8,128)(2,1)} async-done(((bf16[128,1088]{0,1:T(8,128)(2,1)}), bf16[1024,1088]{0,1:T(8,128)(2,1)}) %all-gather.16.cloned.1.call-update) | async-done | bytes 2228240 | tf_op jit(solution)/shard_map/all_gather | solution.py:228
  272.4 29.3 %all-gather.30.cloned.1.call-done = bf16[1024,1088]{0,1:T(8,128)(2,1)} async-done(((bf16[128,1088]{0,1:T(8,128)(2,1)}), bf16[1024,1088]{0,1:T(8,128)(2,1)}) %all-gather.30.cloned.1.call-update) | async-done | bytes 2228240 | tf_op jit(solution)/shard_map/all_gather | solution.py:229
  304.8 29.3 %all-gather.28.cloned.1.call-done = bf16[1024,1088]{0,1:T(8,128)(2,1)} async-done(((bf16[128,1088]{0,1:T(8,128)(2,1)}), bf16[1024,1088]{0,1:T(8,128)(2,1)}) %all-gather.28.cloned.1.call-update) | async-done | bytes 2228240 | tf_op jit(solution)/shard_map/all_gather | solution.py:228
  352.9 21.3 %all-gather.20.cloned.1.call-done = bf16[1088,1088]{1,0:T(8,128)(2,1)} async-done(((bf16[272,1088]{1,0:T(8,128)(2,1)}), bf16[1088,1088]{1,0:T(8,128)(2,1)}) %all-gather.20.cloned.1.call-update) | async-done | bytes 2367504 | tf_op jit(solution)/shard_map/all_gather | solution.py:166
  397.0 75.6 %all-gather.22.cloned.1.call-done = bf16[1088,4352]{1,0:T(8,128)(2,1)} async-done(((bf16[272,4352]{1,0:T(8,128)(2,1)}), bf16[1088,4352]{1,0:T(8,128)(2,1)}) %all-gather.22.cloned.1.call-update) | async-done | bytes 9469968 | tf_op jit(solution)/shard_map/all_gather | solution.py:167
  479.4 96.3 %all-gather.26.cloned.1.call-done = bf16[4352,1088]{1,0:T(8,128)(2,1)} async-done(((bf16[1088,1088]{1,0:T(8,128)(2,1)}), bf16[4352,1088]{1,0:T(8,128)(2,1)}) %all-gather.26.cloned.1.call-update) | async-done | bytes 9469968 | tf_op jit(solution)/shard_map/all_gather | solution.py:168
  607.9 188.6 %while.74 = (s32[]{:T(128)}, f32[4,128,1088]{1,2,0:T(8,128)S(1)}, f32[128,17,64]{0,2,1:T(8,128)}, s32[128]{0:T(128)S(1)}, s32[]{:T(128)}, /*index=5*/s32[1,1,8]{...) while((s32[]{:T(128)}, f32[4,128,1088]{1,2,0:T(8,128)S(1)}, ...), condition=%wide.region_31.32_spmd.clone, body=%wide.region_28.31_spmd.clone.sunk | while | flops 183608976 | bytes 42671764 | solution.py:329
  615.5 14.6 collective-permute-done
  639.0 14.6 collective-permute-done
  805.3 204.7 %while.75 = (s32[]{:T(128)}, f32[4,128,1088]{1,2,0:T(8,128)S(1)}, f32[128,17,64]{0,2,1:T(8,128)}, s32[128]{0:T(128)S(1)}, s32[]{:T(128)}, /*index=5*/s32[1,1,8]{...) while((s32[]{:T(128)}, f32[4,128,1088]{1,2,0:T(8,128)S(1)}, ...), condition=%wide.region_39.40_spmd.clone, body=%wide.region_36.39_spmd.clone.sunk | while | flops 183608976 | bytes 40443484 | solution.py:329
  812.2 34.5 %collective-permute-done.1 = bf16[4,128,1088]{1,2,0:T(8,128)(2,1)} collective-permute-done((bf16[4,128,1088]{1,2,0:T(8,128)(2,1)S(1)}, bf16[4,128,1088]{1,2,0:T(8,128)(2,1)}, u32[]{:S(2)}, u32[]{:S(2)}) %collective-permute-start.1) | collective-permute-done | bytes 1114144 | tf_op jit(solution)/shard_map/while/body/eval_jaxpr/ppermute | solution.py:18
  854.6 15.2 %collective-permute-done.1 = bf16[4,128,1088]{1,2,0:T(8,128)(2,1)} collective-permute-done((bf16[4,128,1088]{1,2,0:T(8,128)(2,1)S(1)}, bf16[4,128,1088]{1,2,0:T(8,128)(2,1)}, u32[]{:S(2)}, u32[]{:S(2)}) %collective-permute-start.1) | collective-permute-done | bytes 1114144 | tf_op jit(solution)/shard_map/while/body/eval_jaxpr/ppermute | solution.py:18
  877.8 15.2 %collective-permute-done.1 = bf16[4,128,1088]{1,2,0:T(8,128)(2,1)} collective-permute-done((bf16[4,128,1088]{1,2,0:T(8,128)(2,1)S(1)}, bf16[4,128,1088]{1,2,0:T(8,128)(2,1)}, u32[]{:S(2)}, u32[]{:S(2)}) %collective-permute-start.1) | collective-permute-done | bytes 1114144 | tf_op jit(solution)/shard_map/while/body/eval_jaxpr/ppermute | solution.py:18
  900.9 15.2 %collective-permute-done.1 = bf16[4,128,1088]{1,2,0:T(8,128)(2,1)} collective-permute-done((bf16[4,128,1088]{1,2,0:T(8,128)(2,1)S(1)}, bf16[4,128,1088]{1,2,0:T(8,128)(2,1)}, u32[]{:S(2)}, u32[]{:S(2)}) %collective-permute-start.1) | collective-permute-done | bytes 1114144 | tf_op jit(solution)/shard_map/while/body/eval_jaxpr/ppermute | solution.py:18
  924.0 15.2 %collective-permute-done.1 = bf16[4,128,1088]{1,2,0:T(8,128)(2,1)} collective-permute-done((bf16[4,128,1088]{1,2,0:T(8,128)(2,1)S(1)}, bf16[4,128,1088]{1,2,0:T(8,128)(2,1)}, u32[]{:S(2)}, u32[]{:S(2)}) %collective-permute-start.1) | collective-permute-done | bytes 1114144 | tf_op jit(solution)/shard_map/while/body/eval_jaxpr/ppermute | solution.py:18
  947.1 15.2 %collective-permute-done.1 = bf16[4,128,1088]{1,2,0:T(8,128)(2,1)} collective-permute-done((bf16[4,128,1088]{1,2,0:T(8,128)(2,1)S(1)}, bf16[4,128,1088]{1,2,0:T(8,128)(2,1)}, u32[]{:S(2)}, u32[]{:S(2)}) %collective-permute-start.1) | collective-permute-done | bytes 1114144 | tf_op jit(solution)/shard_map/while/body/eval_jaxpr/ppermute | solution.py:18
  970.3 15.2 %collective-permute-done.1 = bf16[4,128,1088]{1,2,0:T(8,128)(2,1)} collective-permute-done((bf16[4,128,1088]{1,2,0:T(8,128)(2,1)S(1)}, bf16[4,128,1088]{1,2,0:T(8,128)(2,1)}, u32[]{:S(2)}, u32[]{:S(2)}) %collective-permute-start.1) | collective-permute-done | bytes 1114144 | tf_op jit(solution)/shard_map/while/body/eval_jaxpr/ppermute | solution.py:18
  993.4 15.2 %collective-permute-done.1 = bf16[4,128,1088]{1,2,0:T(8,128)(2,1)} collective-permute-done((bf16[4,128,1088]{1,2,0:T(8,128)(2,1)S(1)}, bf16[4,128,1088]{1,2,0:T(8,128)(2,1)}, u32[]{:S(2)}, u32[]{:S(2)}) %collective-permute-start.1) | collective-permute-done | bytes 1114144 | tf_op jit(solution)/shard_map/while/body/eval_jaxpr/ppermute | solution.py:18
  1086.1 25.1 %reduce-scatter.29.cloned.1.call-done = bf16[1088,408]{0,1:T(8,128)(2,1)} async-done(((bf16[1088,3264]{0,1:T(8,128)(2,1)}), bf16[1088,408]{0,1:T(8,128)(2,1)}) %reduce-scatter.29.cloned.1.call-update) | async-done | bytes 887824
  1119.5 15.9 %all-reduce.12 = (bf16[1088]{0:T(1024)(128)(2,1)S(1)}, bf16[1088]{0:T(1024)(128)(2,1)S(1)}, bf16[1088]{0:T(1024)(128)(2,1)S(1)}, bf16[1088]{0:T(1024)(128)(2,1)S(1)}) all-reduce(bf16[1088]{0:T(1024)(128)(2,1)S(1)} %add_convert_fusion.5, bf16[1088]{0:T(1024)(128)(2,1)S(1)} %add_convert_fusion.4, ...), channel_id=10, replica_groups=mesh['dp'=4,'seq'=8] {'dp'}, use_global_device_ids=true, to_apply=%region_52.53.clone | all-reduce | flops 4352 | bytes 17408
  1135.8 15.6 %all-reduce.11 = (f32[272]{0:T(512)}, f32[272]{0:T(512)}, f32[272]{0:T(512)}, f32[272]{0:T(512)}) all-reduce(f32[272]{0:T(512)S(1)} %dynamic-slice_convert_fusion.4, f32[272]{0:T(512)S(1)} %dynamic-slice_convert_fusion.3, f32[272]{0:T(512)S(1)} %dynamic-slice_convert_fusion.2, ...), channel_id=1, replica_groups=mesh['dp'=4,'seq'=8] {'seq'}, use_global_device_ids=true, to_apply=%region_53.54 | all-reduce | flops 1088 | bytes 8704 | tf_op jit(solution)/shard_map/psum | solution.py:388
  1151.3 66.1 %reduce-scatter.19.cloned.1.call-done = bf16[1088,544]{0,1:T(8,128)(2,1)} async-done(((bf16[1088,4352]{0,1:T(8,128)(2,1)}), bf16[1088,544]{0,1:T(8,128)(2,1)}) %reduce-scatter.19.cloned.1.call-update) | async-done | bytes 1183760 | tf_op jit(solution)/shard_map/reduce_scatter | solution.py:355
  1225.6 92.6 %reduce-scatter.21.cloned.1.call-done = bf16[4352,136]{0,1:T(8,128)(2,1)} async-done(((bf16[4352,1088]{0,1:T(8,128)(2,1)}), bf16[4352,136]{0,1:T(8,128)(2,1)}) %reduce-scatter.21.cloned.1.call-update) | async-done | bytes 1183760 | tf_op jit(solution)/shard_map/reduce_scatter | solution.py:358
  1346.9 29.2 %reduce-scatter.23.cloned.1.call-done = bf16[272,408]{1,0:T(8,128)(2,1)} async-done(((bf16[1088,408]{1,0:T(8,128)(2,1)}), bf16[272,408]{1,0:T(8,128)(2,1)}) %reduce-scatter.23.cloned.1.call-update) | async-done | bytes 221968
  1378.2 56.7 %all-reduce.16.cloned.1.call-done = bf16[1088,544]{0,1:T(8,128)(2,1)} async-done(((bf16[1088,544]{0,1:T(8,128)(2,1)}), bf16[1088,544]{0,1:T(8,128)(2,1)}) %all-reduce.16.cloned.1.call-update) | async-done | bytes 1183760
  1437.4 37.5 %reduce-scatter.27.cloned.1.call-done = bf16[1088,136]{1,0:T(8,128)(2,1)} async-done(((bf16[4352,136]{1,0:T(8,128)(2,1)}), bf16[1088,136]{1,0:T(8,128)(2,1)}) %reduce-scatter.27.cloned.1.call-update) | async-done | bytes 295952
  (874 shorter events, 525.7 us)
Async XLA Ops:
  7.2 35.4 %all-gather.32.cloned.1.call-start = ((), (), s32[]{:S(2)}) async-start(), calls=%async_computation.18 | async-start | bytes 2506752 | tf_op jit(solution)/shard_map/all_gather | solution.py:159
  7.9 119.7 %all-gather.14.cloned.1.call-start = ((), (), s32[]{:S(2)}) async-start(), calls=%async_computation.7 | async-start | bytes 9052160 | tf_op jit(solution)/shard_map/all_gather | solution.py:165
  49.7 121.5 %all-gather.34.cloned.1.call-start = ((), (), s32[]{:S(2)}) async-start(), calls=%async_computation.19 | async-start | bytes 3133440 | tf_op jit(solution)/shard_map/all_gather | solution.py:161
  50.5 154.1 %all-gather.24.cloned.1.call-start = ((), (), s32[]{:S(2)}) async-start(), calls=%async_computation.12 | async-start | bytes 2820096 | tf_op jit(solution)/shard_map/all_gather | solution.py:162
  51.1 185.9 %all-gather.18.cloned.1.call-start = ((), (), s32[]{:S(2)}) async-start(), calls=%async_computation.9 | async-start | bytes 2506752 | tf_op jit(solution)/shard_map/all_gather | solution.py:229
  135.2 134.0 %all-gather.16.cloned.1.call-start = ((), (), s32[]{:S(2)}) async-start(), calls=%async_computation.8 | async-start | bytes 2506752 | tf_op jit(solution)/shard_map/all_gather | solution.py:228
  135.8 165.9 %all-gather.30.cloned.1.call-start = ((), (), s32[]{:S(2)}) async-start(), calls=%async_computation.15 | async-start | bytes 2506752 | tf_op jit(solution)/shard_map/all_gather | solution.py:229
  144.0 190.1 %all-gather.28.cloned.1.call-start = ((), (), s32[]{:S(2)}) async-start(), calls=%async_computation.14 | async-start | bytes 2506752 | tf_op jit(solution)/shard_map/all_gather | solution.py:228
  144.8 229.5 %all-gather.20.cloned.1.call-start = ((), (), s32[]{:S(2)}) async-start(), calls=%async_computation.10 | async-start | bytes 3133440 | tf_op jit(solution)/shard_map/all_gather | solution.py:166
  167.1 305.5 %all-gather.22.cloned.1.call-start = ((), (), s32[]{:S(2)}) async-start(), calls=%async_computation.11 | async-start | bytes 11837440 | tf_op jit(solution)/shard_map/all_gather | solution.py:167
  180.8 394.9 %all-gather.26.cloned.1.call-start = ((), (), s32[]{:S(2)}) async-start(), calls=%async_computation.13 | async-start | bytes 12533760 | tf_op jit(solution)/shard_map/all_gather | solution.py:168
  209.8 868.2 %reduce-scatter.31.cloned.1.call-start = ((), (), s32[]{:S(2)}) async-start(), calls=%async_computation.25 | async-start | bytes 2820096
  613.2 16.9 %collective-permute-start = (bf16[4,128,1088]{1,2,0:T(8,128)(2,1)S(1)}, bf16[4,128,1088]{1,2,0:T(8,128)(2,1)}, u32[]{:S(2)}, u32[]{:S(2)}) collective-permute-start(bf16[4,128,1088]{1,2,0:T(8,128)(2,1)S(1)} %pad_maximum_fusion.12), channel_id=1, source_target_pairs={{7,0},{0,1},{1,2},{2,3},{3,4},{4,5},{5,6},{6,7},{15,8},{8,9},{9,10... | collective-permute-start | bytes 3342344 | tf_op jit(solution)/shard_map/while/body/eval_jaxpr/ppermute | solution.py:18
  636.8 16.9 %collective-permute-start = (bf16[4,128,1088]{1,2,0:T(8,128)(2,1)S(1)}, bf16[4,128,1088]{1,2,0:T(8,128)(2,1)}, u32[]{:S(2)}, u32[]{:S(2)}) collective-permute-start(bf16[4,128,1088]{1,2,0:T(8,128)(2,1)S(1)} %pad_maximum_fusion.12), channel_id=1, source_target_pairs={{7,0},{0,1},{1,2},{2,3},{3,4},{4,5},{5,6},{6,7},{15,8},{8,9},{9,10... | collective-permute-start | bytes 3342344 | tf_op jit(solution)/shard_map/while/body/eval_jaxpr/ppermute | solution.py:18
  660.3 16.9 %collective-permute-start = (bf16[4,128,1088]{1,2,0:T(8,128)(2,1)S(1)}, bf16[4,128,1088]{1,2,0:T(8,128)(2,1)}, u32[]{:S(2)}, u32[]{:S(2)}) collective-permute-start(bf16[4,128,1088]{1,2,0:T(8,128)(2,1)S(1)} %pad_maximum_fusion.12), channel_id=1, source_target_pairs={{7,0},{0,1},{1,2},{2,3},{3,4},{4,5},{5,6},{6,7},{15,8},{8,9},{9,10... | collective-permute-start | bytes 3342344 | tf_op jit(solution)/shard_map/while/body/eval_jaxpr/ppermute | solution.py:18
  683.9 16.9 %collective-permute-start = (bf16[4,128,1088]{1,2,0:T(8,128)(2,1)S(1)}, bf16[4,128,1088]{1,2,0:T(8,128)(2,1)}, u32[]{:S(2)}, u32[]{:S(2)}) collective-permute-start(bf16[4,128,1088]{1,2,0:T(8,128)(2,1)S(1)} %pad_maximum_fusion.12), channel_id=1, source_target_pairs={{7,0},{0,1},{1,2},{2,3},{3,4},{4,5},{5,6},{6,7},{15,8},{8,9},{9,10... | collective-permute-start | bytes 3342344 | tf_op jit(solution)/shard_map/while/body/eval_jaxpr/ppermute | solution.py:18
  707.5 16.9 %collective-permute-start = (bf16[4,128,1088]{1,2,0:T(8,128)(2,1)S(1)}, bf16[4,128,1088]{1,2,0:T(8,128)(2,1)}, u32[]{:S(2)}, u32[]{:S(2)}) collective-permute-start(bf16[4,128,1088]{1,2,0:T(8,128)(2,1)S(1)} %pad_maximum_fusion.12), channel_id=1, source_target_pairs={{7,0},{0,1},{1,2},{2,3},{3,4},{4,5},{5,6},{6,7},{15,8},{8,9},{9,10... | collective-permute-start | bytes 3342344 | tf_op jit(solution)/shard_map/while/body/eval_jaxpr/ppermute | solution.py:18
  731.0 16.9 %collective-permute-start = (bf16[4,128,1088]{1,2,0:T(8,128)(2,1)S(1)}, bf16[4,128,1088]{1,2,0:T(8,128)(2,1)}, u32[]{:S(2)}, u32[]{:S(2)}) collective-permute-start(bf16[4,128,1088]{1,2,0:T(8,128)(2,1)S(1)} %pad_maximum_fusion.12), channel_id=1, source_target_pairs={{7,0},{0,1},{1,2},{2,3},{3,4},{4,5},{5,6},{6,7},{15,8},{8,9},{9,10... | collective-permute-start | bytes 3342344 | tf_op jit(solution)/shard_map/while/body/eval_jaxpr/ppermute | solution.py:18
  754.6 16.9 %collective-permute-start = (bf16[4,128,1088]{1,2,0:T(8,128)(2,1)S(1)}, bf16[4,128,1088]{1,2,0:T(8,128)(2,1)}, u32[]{:S(2)}, u32[]{:S(2)}) collective-permute-start(bf16[4,128,1088]{1,2,0:T(8,128)(2,1)S(1)} %pad_maximum_fusion.12), channel_id=1, source_target_pairs={{7,0},{0,1},{1,2},{2,3},{3,4},{4,5},{5,6},{6,7},{15,8},{8,9},{9,10... | collective-permute-start | bytes 3342344 | tf_op jit(solution)/shard_map/while/body/eval_jaxpr/ppermute | solution.py:18
  803.7 307.5 %reduce-scatter.29.cloned.1.call-start = ((), (), s32[]{:S(2)}) async-start(), calls=%async_computation.24 | async-start | bytes 8460288
  810.5 36.2 %collective-permute-start.1 = (bf16[4,128,1088]{1,2,0:T(8,128)(2,1)S(1)}, bf16[4,128,1088]{1,2,0:T(8,128)(2,1)}, u32[]{:S(2)}, u32[]{:S(2)}) collective-permute-start(bf16[4,128,1088]{1,2,0:T(8,128)(2,1)S(1)} %pad_maximum_fusion.13), channel_id=1, source_target_pairs={{7,0},{0,1},{1,2},{2,3},{3,4},{4,5},{5,6},{6,7},{15,8},{8,9},{9,10... | collective-permute-start | bytes 3342344 | tf_op jit(solution)/shard_map/while/body/eval_jaxpr/ppermute | solution.py:18
  852.9 16.9 %collective-permute-start.1 = (bf16[4,128,1088]{1,2,0:T(8,128)(2,1)S(1)}, bf16[4,128,1088]{1,2,0:T(8,128)(2,1)}, u32[]{:S(2)}, u32[]{:S(2)}) collective-permute-start(bf16[4,128,1088]{1,2,0:T(8,128)(2,1)S(1)} %pad_maximum_fusion.13), channel_id=1, source_target_pairs={{7,0},{0,1},{1,2},{2,3},{3,4},{4,5},{5,6},{6,7},{15,8},{8,9},{9,10... | collective-permute-start | bytes 3342344 | tf_op jit(solution)/shard_map/while/body/eval_jaxpr/ppermute | solution.py:18
  876.0 16.9 %collective-permute-start.1 = (bf16[4,128,1088]{1,2,0:T(8,128)(2,1)S(1)}, bf16[4,128,1088]{1,2,0:T(8,128)(2,1)}, u32[]{:S(2)}, u32[]{:S(2)}) collective-permute-start(bf16[4,128,1088]{1,2,0:T(8,128)(2,1)S(1)} %pad_maximum_fusion.13), channel_id=1, source_target_pairs={{7,0},{0,1},{1,2},{2,3},{3,4},{4,5},{5,6},{6,7},{15,8},{8,9},{9,10... | collective-permute-start | bytes 3342344 | tf_op jit(solution)/shard_map/while/body/eval_jaxpr/ppermute | solution.py:18
  899.2 16.9 %collective-permute-start.1 = (bf16[4,128,1088]{1,2,0:T(8,128)(2,1)S(1)}, bf16[4,128,1088]{1,2,0:T(8,128)(2,1)}, u32[]{:S(2)}, u32[]{:S(2)}) collective-permute-start(bf16[4,128,1088]{1,2,0:T(8,128)(2,1)S(1)} %pad_maximum_fusion.13), channel_id=1, source_target_pairs={{7,0},{0,1},{1,2},{2,3},{3,4},{4,5},{5,6},{6,7},{15,8},{8,9},{9,10... | collective-permute-start | bytes 3342344 | tf_op jit(solution)/shard_map/while/body/eval_jaxpr/ppermute | solution.py:18
  922.3 16.9 %collective-permute-start.1 = (bf16[4,128,1088]{1,2,0:T(8,128)(2,1)S(1)}, bf16[4,128,1088]{1,2,0:T(8,128)(2,1)}, u32[]{:S(2)}, u32[]{:S(2)}) collective-permute-start(bf16[4,128,1088]{1,2,0:T(8,128)(2,1)S(1)} %pad_maximum_fusion.13), channel_id=1, source_target_pairs={{7,0},{0,1},{1,2},{2,3},{3,4},{4,5},{5,6},{6,7},{15,8},{8,9},{9,10... | collective-permute-start | bytes 3342344 | tf_op jit(solution)/shard_map/while/body/eval_jaxpr/ppermute | solution.py:18
  945.4 16.9 %collective-permute-start.1 = (bf16[4,128,1088]{1,2,0:T(8,128)(2,1)S(1)}, bf16[4,128,1088]{1,2,0:T(8,128)(2,1)}, u32[]{:S(2)}, u32[]{:S(2)}) collective-permute-start(bf16[4,128,1088]{1,2,0:T(8,128)(2,1)S(1)} %pad_maximum_fusion.13), channel_id=1, source_target_pairs={{7,0},{0,1},{1,2},{2,3},{3,4},{4,5},{5,6},{6,7},{15,8},{8,9},{9,10... | collective-permute-start | bytes 3342344 | tf_op jit(solution)/shard_map/while/body/eval_jaxpr/ppermute | solution.py:18
  1031.5 186.0 %reduce-scatter.19.cloned.1.call-start = ((), (), s32[]{:S(2)}) async-start(), calls=%async_computation.16 | async-start | bytes 11280384 | tf_op jit(solution)/shard_map/reduce_scatter | solution.py:355
  1054.6 263.6 %reduce-scatter.21.cloned.1.call-start = ((), (), s32[]{:S(2)}) async-start(), calls=%async_computation.17 | async-start | bytes 10653696 | tf_op jit(solution)/shard_map/reduce_scatter | solution.py:358
  1077.3 267.8 %reduce-scatter.25.cloned.1.call-start = ((), (), s32[]{:S(2)}) async-start(), calls=%async_computation.21 | async-start | bytes 696320
  1080.0 296.1 %reduce-scatter.23.cloned.1.call-start = ((), (), s32[]{:S(2)}) async-start(), calls=%async_computation.20 | async-start | bytes 1392640
  1113.5 321.5 %all-reduce.16.cloned.1.call-start = ((), (), s32[]{:S(2)}) async-start(), calls=%async_computation.23 | async-start | bytes 2506752
  1217.5 257.4 %reduce-scatter.27.cloned.1.call-start = ((), (), s32[]{:S(2)}) async-start(), calls=%async_computation.22 | async-start | bytes 2785280
  (197 other events, 1155.4 us)
Sparse Core Ops, SparseCore 0:
  9.7 32.8 all-gather.31
  49.9 77.6 all-gather.13
  129.2 41.9 all-gather.33
  172.7 31.8 all-gather.23
  206.0 30.8 all-gather.17
  238.4 30.7 all-gather.15
  270.8 30.7 all-gather.29
  303.2 30.7 all-gather.27
  336.5 37.6 all-gather.19
  375.9 96.6 all-gather.21
  474.4 101.2 all-gather.25
  803.8 42.2 reduce-scatter.30
  1031.6 79.4 reduce-scatter.28
  1113.4 104.0 reduce-scatter.18
  1219.7 98.4 reduce-scatter.20
  1321.8 23.3 reduce-scatter.24
  1347.9 28.1 reduce-scatter.22
  1379.1 55.7 all-reduce.15
  1438.2 36.5 reduce-scatter.26
where the time goes:
time: 1490 us; the launch traced here: 1480 us
  waiting for transfers between devices  1000 us (67%)
  matrix products  202 us (14%)
  local copies, waits for them, and re-layouts  127 us (9%)
  blocking collectives  68.8 us (5%)
  other arithmetic  59 us (4%)
  between operations  17.7 us (1%)
    ppermute x16, waiting for transfers between devices, from_behind(): return lax.ppermute(block, axis, route)  257 us
    unnamed x25, waiting for transfers between devices  164 us
    all_gather x1, waiting for transfers between devices, shards(): lax.all_gather(col_parts[3], 'dp', axis=0, tiled=True)  96.3 us
    reduce_scatter x1, waiting for transfers between devices, shards(): lax.psum_scatter(sum_down.astype(jnp.bfloat16), 'seq', scatter_dimension=...  92.6 us
    all_gather x1, waiting for transfers between devices, shards(): lax.all_gather(col_parts[2], 'dp', axis=0, tiled=True)  75.6 us
    reduce_scatter x1, waiting for transfers between devices, shards(): lax.psum_scatter(sum_up.astype(jnp.bfloat16), 'seq', scatter_dimension=1,...  66.1 us
    all_gather x2, waiting for transfers between devices, shards(): lax.all_gather(key_local, 'seq', axis=0, tiled=True)  58.4 us
    all_gather x1, waiting for transfers between devices, shards(): lax.all_gather(col_parts[0], 'dp', axis=0, tiled=True)  57.6 us
  transfers between devices with their start and end apart: 35, of which 34 were waited for; matrix products, arithmetic and copies ran while one was open for 16% of the time, Pallas kernels for 0%

commit v1 on v0

--- a/solution.py
+++ b/solution.py
@@ -36,6 +36,11 @@
         - jnp.mean(grad_scaled, -1, keepdims=True)
         - scaled * jnp.mean(grad_scaled * scaled, -1, keepdims=True)
     )
+
+
+def running_total(counts):
+    index = jnp.arange(counts.shape[0], dtype=jnp.int32)
+    return jnp.sum(jnp.where(index[None, :] <= index[:, None], counts[None, :], 0), 1)
 
 
 def segment_of(places, doc_ends):
@@ -172,7 +177,7 @@
             lax.all_gather(bias_two, "dp", axis=0, tiled=True),
         )
         slot_row = slot_order[micro_index, 0]
-        doc_ends = jnp.cumsum(lengths[micro_index, 0])
+        doc_ends = running_total(lengths[micro_index, 0])
         base_slot = jnp.sum(jnp.where(slot_ids == my_slot, slot_row, 0))
         q_place = base_slot * tok_dev + jnp.arange(tok_dev, dtype=jnp.int32)
         q_segment = segment_of(q_place, doc_ends)

time: 1490 us -> 1490 us (level)
  no operation moved by 1% of the time
where the time goes in v1:
time: 1490 us; the launch traced here: 1480 us
  waiting for transfers between devices  1000 us (67%)
  matrix products  202 us (14%)
  local copies, waits for them, and re-layouts  127 us (9%)
  blocking collectives  68.8 us (5%)
  other arithmetic  58.9 us (4%)
  between operations  17.7 us (1%)
    ppermute x16, waiting for transfers between devices, from_behind(): return lax.ppermute(block, axis, route)  257 us
    unnamed x25, waiting for transfers between devices  164 us
    all_gather x1, waiting for transfers between devices, shards(): lax.all_gather(col_parts[3], 'dp', axis=0, tiled=True)  96.3 us
    reduce_scatter x1, waiting for transfers between devices, shards(): lax.psum_scatter(sum_down.astype(jnp.bfloat16), 'seq', scatter_dimension=...  92.6 us
    all_gather x1, waiting for transfers between devices, shards(): lax.all_gather(col_parts[2], 'dp', axis=0, tiled=True)  75.6 us
    reduce_scatter x1, waiting for transfers between devices, shards(): lax.psum_scatter(sum_up.astype(jnp.bfloat16), 'seq', scatter_dimension=1,...  66.1 us
    all_gather x2, waiting for transfers between devices, shards(): lax.all_gather(key_local, 'seq', axis=0, tiled=True)  58.4 us
    all_gather x1, waiting for transfers between devices, shards(): lax.all_gather(col_parts[0], 'dp', axis=0, tiled=True)  57.6 us
  transfers between devices with their start and end apart: 35, of which 34 were waited for; matrix products, arithmetic and copies ran while one was open for 16% of the time, Pallas kernels for 0%

profile of v1, /device:TPU:0, one launch (start us, length us, event | category | flops | bytes accessed | tf_op | source)
XLA Modules:
  0.0 1483.8 jit_solution(6978261043025893272)
XLA Ops:
  8.0 34.6 %all-gather.32.cloned.1.call-done = bf16[8,408,272]{1,2,0:T(8,128)(2,1)} async-done(((bf16[1,408,272]{1,2,0:T(8,128)(2,1)}), bf16[8,408,272]{1,2,0:T(8,128)(2,1)}) %all-gather.32.cloned.1.call-update) | async-done | bytes 1775632 | tf_op jit(solution)/shard_map/all_gather | solution.py:164
  53.4 16.2 %all-reduce.13 = (bf16[1088]{0:T(1024)(128)(2,1)S(1)}, bf16[1088]{0:T(1024)(128)(2,1)S(1)}, bf16[1088]{0:T(1024)(128)(2,1)S(1)}, bf16[1088]{0:T(1024)(128)(2,1)S(1)}) all-reduce(bf16[1088]{0:T(1024)(128)(2,1)S(1)} %dynamic-update-slice.1, bf16[1088]{0:T(1024)(128)(2,1)S(1)} %dynamic-update-slice, ...), channel_id=1, replica_groups=mesh['dp'=4,'seq'=8] {'dp'}, use_global_device_ids=true, to_apply=%add.1 | all-reduce | flops 4352 | bytes 17408
  70.0 57.6 %all-gather.14.cloned.1.call-done = bf16[1088,3264]{1,0:T(8,128)(2,1)} async-done(((bf16[272,3264]{1,0:T(8,128)(2,1)}), bf16[1088,3264]{1,0:T(8,128)(2,1)}) %all-gather.14.cloned.1.call-update) | async-done | bytes 7102480 | tf_op jit(solution)/shard_map/all_gather | solution.py:170
  144.8 21.1 %all_gather.38 = bf16[272,1088]{0,1:T(8,128)(2,1)S(1)} all-gather(bf16[272,136]{0,1:T(8,128)(2,1)S(1)} %copy-done.60), channel_id=1, replica_groups=mesh['dp'=4,'seq'=8] {'seq'}, dimensions={1}, use_global_device_ids=true | all-gather | bytes 665856 | tf_op jit(solution)/shard_map/all_gather | solution.py:165
  184.0 20.6 %all-gather.24.cloned.1.call-done = bf16[1088,1088]{0,1:T(8,128)(2,1)} async-done(((bf16[1088,136]{0,1:T(8,128)(2,1)}), bf16[1088,1088]{0,1:T(8,128)(2,1)}) %all-gather.24.cloned.1.call-update) | async-done | bytes 2367504 | tf_op jit(solution)/shard_map/all_gather | solution.py:167
  213.5 23.4 %all-gather.18.cloned.1.call-done = bf16[1024,1088]{0,1:T(8,128)(2,1)} async-done(((bf16[128,1088]{0,1:T(8,128)(2,1)}), bf16[1024,1088]{0,1:T(8,128)(2,1)}) %all-gather.18.cloned.1.call-update) | async-done | bytes 2228240 | tf_op jit(solution)/shard_map/all_gather | solution.py:234
  240.1 29.1 %all-gather.16.cloned.1.call-done = bf16[1024,1088]{0,1:T(8,128)(2,1)} async-done(((bf16[128,1088]{0,1:T(8,128)(2,1)}), bf16[1024,1088]{0,1:T(8,128)(2,1)}) %all-gather.16.cloned.1.call-update) | async-done | bytes 2228240 | tf_op jit(solution)/shard_map/all_gather | solution.py:233
  272.4 29.3 %all-gather.30.cloned.1.call-done = bf16[1024,1088]{0,1:T(8,128)(2,1)} async-done(((bf16[128,1088]{0,1:T(8,128)(2,1)}), bf16[1024,1088]{0,1:T(8,128)(2,1)}) %all-gather.30.cloned.1.call-update) | async-done | bytes 2228240 | tf_op jit(solution)/shard_map/all_gather | solution.py:234
  304.8 29.3 %all-gather.28.cloned.1.call-done = bf16[1024,1088]{0,1:T(8,128)(2,1)} async-done(((bf16[128,1088]{0,1:T(8,128)(2,1)}), bf16[1024,1088]{0,1:T(8,128)(2,1)}) %all-gather.28.cloned.1.call-update) | async-done | bytes 2228240 | tf_op jit(solution)/shard_map/all_gather | solution.py:233
  352.9 21.3 %all-gather.20.cloned.1.call-done = bf16[1088,1088]{1,0:T(8,128)(2,1)} async-done(((bf16[272,1088]{1,0:T(8,128)(2,1)}), bf16[1088,1088]{1,0:T(8,128)(2,1)}) %all-gather.20.cloned.1.call-update) | async-done | bytes 2367504 | tf_op jit(solution)/shard_map/all_gather | solution.py:171
  397.0 75.6 %all-gather.22.cloned.1.call-done = bf16[1088,4352]{1,0:T(8,128)(2,1)} async-done(((bf16[272,4352]{1,0:T(8,128)(2,1)}), bf16[1088,4352]{1,0:T(8,128)(2,1)}) %all-gather.22.cloned.1.call-update) | async-done | bytes 9469968 | tf_op jit(solution)/shard_map/all_gather | solution.py:172
  479.4 96.3 %all-gather.26.cloned.1.call-done = bf16[4352,1088]{1,0:T(8,128)(2,1)} async-done(((bf16[1088,1088]{1,0:T(8,128)(2,1)}), bf16[4352,1088]{1,0:T(8,128)(2,1)}) %all-gather.26.cloned.1.call-update) | async-done | bytes 9469968 | tf_op jit(solution)/shard_map/all_gather | solution.py:173
  607.9 188.6 %while.74 = (s32[]{:T(128)}, f32[4,128,1088]{1,2,0:T(8,128)S(1)}, f32[128,17,64]{0,2,1:T(8,128)}, s32[128]{0:T(128)S(1)}, s32[]{:T(128)}, /*index=5*/s32[1,1,8]{...) while((s32[]{:T(128)}, f32[4,128,1088]{1,2,0:T(8,128)S(1)}, ...), condition=%wide.region_31.32_spmd.clone, body=%wide.region_28.31_spmd.clone.sunk | while | flops 183608976 | bytes 42671764 | solution.py:334
  615.5 14.6 collective-permute-done
  639.0 14.6 collective-permute-done
  805.3 204.7 %while.75 = (s32[]{:T(128)}, f32[4,128,1088]{1,2,0:T(8,128)S(1)}, f32[128,17,64]{0,2,1:T(8,128)}, s32[128]{0:T(128)S(1)}, s32[]{:T(128)}, /*index=5*/s32[1,1,8]{...) while((s32[]{:T(128)}, f32[4,128,1088]{1,2,0:T(8,128)S(1)}, ...), condition=%wide.region_39.40_spmd.clone, body=%wide.region_36.39_spmd.clone.sunk | while | flops 183608976 | bytes 40443484 | solution.py:334
  812.2 34.5 %collective-permute-done.1 = bf16[4,128,1088]{1,2,0:T(8,128)(2,1)} collective-permute-done((bf16[4,128,1088]{1,2,0:T(8,128)(2,1)S(1)}, bf16[4,128,1088]{1,2,0:T(8,128)(2,1)}, u32[]{:S(2)}, u32[]{:S(2)}) %collective-permute-start.1) | collective-permute-done | bytes 1114144 | tf_op jit(solution)/shard_map/while/body/eval_jaxpr/ppermute | solution.py:18
  854.6 15.2 %collective-permute-done.1 = bf16[4,128,1088]{1,2,0:T(8,128)(2,1)} collective-permute-done((bf16[4,128,1088]{1,2,0:T(8,128)(2,1)S(1)}, bf16[4,128,1088]{1,2,0:T(8,128)(2,1)}, u32[]{:S(2)}, u32[]{:S(2)}) %collective-permute-start.1) | collective-permute-done | bytes 1114144 | tf_op jit(solution)/shard_map/while/body/eval_jaxpr/ppermute | solution.py:18
  877.8 15.2 %collective-permute-done.1 = bf16[4,128,1088]{1,2,0:T(8,128)(2,1)} collective-permute-done((bf16[4,128,1088]{1,2,0:T(8,128)(2,1)S(1)}, bf16[4,128,1088]{1,2,0:T(8,128)(2,1)}, u32[]{:S(2)}, u32[]{:S(2)}) %collective-permute-start.1) | collective-permute-done | bytes 1114144 | tf_op jit(solution)/shard_map/while/body/eval_jaxpr/ppermute | solution.py:18
  900.9 15.2 %collective-permute-done.1 = bf16[4,128,1088]{1,2,0:T(8,128)(2,1)} collective-permute-done((bf16[4,128,1088]{1,2,0:T(8,128)(2,1)S(1)}, bf16[4,128,1088]{1,2,0:T(8,128)(2,1)}, u32[]{:S(2)}, u32[]{:S(2)}) %collective-permute-start.1) | collective-permute-done | bytes 1114144 | tf_op jit(solution)/shard_map/while/body/eval_jaxpr/ppermute | solution.py:18
  924.0 15.2 %collective-permute-done.1 = bf16[4,128,1088]{1,2,0:T(8,128)(2,1)} collective-permute-done((bf16[4,128,1088]{1,2,0:T(8,128)(2,1)S(1)}, bf16[4,128,1088]{1,2,0:T(8,128)(2,1)}, u32[]{:S(2)}, u32[]{:S(2)}) %collective-permute-start.1) | collective-permute-done | bytes 1114144 | tf_op jit(solution)/shard_map/while/body/eval_jaxpr/ppermute | solution.py:18
  947.1 15.2 %collective-permute-done.1 = bf16[4,128,1088]{1,2,0:T(8,128)(2,1)} collective-permute-done((bf16[4,128,1088]{1,2,0:T(8,128)(2,1)S(1)}, bf16[4,128,1088]{1,2,0:T(8,128)(2,1)}, u32[]{:S(2)}, u32[]{:S(2)}) %collective-permute-start.1) | collective-permute-done | bytes 1114144 | tf_op jit(solution)/shard_map/while/body/eval_jaxpr/ppermute | solution.py:18
  970.3 15.2 %collective-permute-done.1 = bf16[4,128,1088]{1,2,0:T(8,128)(2,1)} collective-permute-done((bf16[4,128,1088]{1,2,0:T(8,128)(2,1)S(1)}, bf16[4,128,1088]{1,2,0:T(8,128)(2,1)}, u32[]{:S(2)}, u32[]{:S(2)}) %collective-permute-start.1) | collective-permute-done | bytes 1114144 | tf_op jit(solution)/shard_map/while/body/eval_jaxpr/ppermute | solution.py:18
  993.4 15.2 %collective-permute-done.1 = bf16[4,128,1088]{1,2,0:T(8,128)(2,1)} collective-permute-done((bf16[4,128,1088]{1,2,0:T(8,128)(2,1)S(1)}, bf16[4,128,1088]{1,2,0:T(8,128)(2,1)}, u32[]{:S(2)}, u32[]{:S(2)}) %collective-permute-start.1) | collective-permute-done | bytes 1114144 | tf_op jit(solution)/shard_map/while/body/eval_jaxpr/ppermute | solution.py:18
  1086.1 25.1 %reduce-scatter.29.cloned.1.call-done = bf16[1088,408]{0,1:T(8,128)(2,1)} async-done(((bf16[1088,3264]{0,1:T(8,128)(2,1)}), bf16[1088,408]{0,1:T(8,128)(2,1)}) %reduce-scatter.29.cloned.1.call-update) | async-done | bytes 887824
  1119.5 15.9 %all-reduce.12 = (bf16[1088]{0:T(1024)(128)(2,1)S(1)}, bf16[1088]{0:T(1024)(128)(2,1)S(1)}, bf16[1088]{0:T(1024)(128)(2,1)S(1)}, bf16[1088]{0:T(1024)(128)(2,1)S(1)}) all-reduce(bf16[1088]{0:T(1024)(128)(2,1)S(1)} %add_convert_fusion.5, bf16[1088]{0:T(1024)(128)(2,1)S(1)} %add_convert_fusion.4, ...), channel_id=10, replica_groups=mesh['dp'=4,'seq'=8] {'dp'}, use_global_device_ids=true, to_apply=%region_52.53.clone | all-reduce | flops 4352 | bytes 17408
  1135.8 15.6 %all-reduce.11 = (f32[272]{0:T(512)}, f32[272]{0:T(512)}, f32[272]{0:T(512)}, f32[272]{0:T(512)}) all-reduce(f32[272]{0:T(512)S(1)} %dynamic-slice_convert_fusion.4, f32[272]{0:T(512)S(1)} %dynamic-slice_convert_fusion.3, f32[272]{0:T(512)S(1)} %dynamic-slice_convert_fusion.2, ...), channel_id=1, replica_groups=mesh['dp'=4,'seq'=8] {'seq'}, use_global_device_ids=true, to_apply=%region_53.54 | all-reduce | flops 1088 | bytes 8704 | tf_op jit(solution)/shard_map/psum | solution.py:393
  1151.3 66.1 %reduce-scatter.19.cloned.1.call-done = bf16[1088,544]{0,1:T(8,128)(2,1)} async-done(((bf16[1088,4352]{0,1:T(8,128)(2,1)}), bf16[1088,544]{0,1:T(8,128)(2,1)}) %reduce-scatter.19.cloned.1.call-update) | async-done | bytes 1183760 | tf_op jit(solution)/shard_map/reduce_scatter | solution.py:360
  1225.6 92.6 %reduce-scatter.21.cloned.1.call-done = bf16[4352,136]{0,1:T(8,128)(2,1)} async-done(((bf16[4352,1088]{0,1:T(8,128)(2,1)}), bf16[4352,136]{0,1:T(8,128)(2,1)}) %reduce-scatter.21.cloned.1.call-update) | async-done | bytes 1183760 | tf_op jit(solution)/shard_map/reduce_scatter | solution.py:363
  1346.9 29.2 %reduce-scatter.23.cloned.1.call-done = bf16[272,408]{1,0:T(8,128)(2,1)} async-done(((bf16[1088,408]{1,0:T(8,128)(2,1)}), bf16[272,408]{1,0:T(8,128)(2,1)}) %reduce-scatter.23.cloned.1.call-update) | async-done | bytes 221968
  1378.2 56.7 %all-reduce.16.cloned.1.call-done = bf16[1088,544]{0,1:T(8,128)(2,1)} async-done(((bf16[1088,544]{0,1:T(8,128)(2,1)}), bf16[1088,544]{0,1:T(8,128)(2,1)}) %all-reduce.16.cloned.1.call-update) | async-done | bytes 1183760
  1437.4 37.5 %reduce-scatter.27.cloned.1.call-done = bf16[1088,136]{1,0:T(8,128)(2,1)} async-done(((bf16[4352,136]{1,0:T(8,128)(2,1)}), bf16[1088,136]{1,0:T(8,128)(2,1)}) %reduce-scatter.27.cloned.1.call-update) | async-done | bytes 295952
  (874 shorter events, 525.6 us)
Async XLA Ops:
  7.2 35.4 %all-gather.32.cloned.1.call-start = ((), (), s32[]{:S(2)}) async-start(), calls=%async_computation.18 | async-start | bytes 2506752 | tf_op jit(solution)/shard_map/all_gather | solution.py:164
  7.9 119.7 %all-gather.14.cloned.1.call-start = ((), (), s32[]{:S(2)}) async-start(), calls=%async_computation.7 | async-start | bytes 9052160 | tf_op jit(solution)/shard_map/all_gather | solution.py:170
  49.7 121.5 %all-gather.34.cloned.1.call-start = ((), (), s32[]{:S(2)}) async-start(), calls=%async_computation.19 | async-start | bytes 3133440 | tf_op jit(solution)/shard_map/all_gather | solution.py:166
  50.5 154.1 %all-gather.24.cloned.1.call-start = ((), (), s32[]{:S(2)}) async-start(), calls=%async_computation.12 | async-start | bytes 2820096 | tf_op jit(solution)/shard_map/all_gather | solution.py:167
  51.1 185.9 %all-gather.18.cloned.1.call-start = ((), (), s32[]{:S(2)}) async-start(), calls=%async_computation.9 | async-start | bytes 2506752 | tf_op jit(solution)/shard_map/all_gather | solution.py:234
  135.2 134.0 %all-gather.16.cloned.1.call-start = ((), (), s32[]{:S(2)}) async-start(), calls=%async_computation.8 | async-start | bytes 2506752 | tf_op jit(solution)/shard_map/all_gather | solution.py:233
  135.8 165.9 %all-gather.30.cloned.1.call-start = ((), (), s32[]{:S(2)}) async-start(), calls=%async_computation.15 | async-start | bytes 2506752 | tf_op jit(solution)/shard_map/all_gather | solution.py:234
  144.0 190.1 %all-gather.28.cloned.1.call-start = ((), (), s32[]{:S(2)}) async-start(), calls=%async_computation.14 | async-start | bytes 2506752 | tf_op jit(solution)/shard_map/all_gather | solution.py:233
  144.8 229.5 %all-gather.20.cloned.1.call-start = ((), (), s32[]{:S(2)}) async-start(), calls=%async_computation.10 | async-start | bytes 3133440 | tf_op jit(solution)/shard_map/all_gather | solution.py:171
  167.1 305.5 %all-gather.22.cloned.1.call-start = ((), (), s32[]{:S(2)}) async-start(), calls=%async_computation.11 | async-start | bytes 11837440 | tf_op jit(solution)/shard_map/all_gather | solution.py:172
  180.8 394.9 %all-gather.26.cloned.1.call-start = ((), (), s32[]{:S(2)}) async-start(), calls=%async_computation.13 | async-start | bytes 12533760 | tf_op jit(solution)/shard_map/all_gather | solution.py:173
  209.8 868.2 %reduce-scatter.31.cloned.1.call-start = ((), (), s32[]{:S(2)}) async-start(), calls=%async_computation.25 | async-start | bytes 2820096
  613.2 16.9 %collective-permute-start = (bf16[4,128,1088]{1,2,0:T(8,128)(2,1)S(1)}, bf16[4,128,1088]{1,2,0:T(8,128)(2,1)}, u32[]{:S(2)}, u32[]{:S(2)}) collective-permute-start(bf16[4,128,1088]{1,2,0:T(8,128)(2,1)S(1)} %pad_maximum_fusion.12), channel_id=1, source_target_pairs={{7,0},{0,1},{1,2},{2,3},{3,4},{4,5},{5,6},{6,7},{15,8},{8,9},{9,10... | collective-permute-start | bytes 3342344 | tf_op jit(solution)/shard_map/while/body/eval_jaxpr/ppermute | solution.py:18
  636.8 16.9 %collective-permute-start = (bf16[4,128,1088]{1,2,0:T(8,128)(2,1)S(1)}, bf16[4,128,1088]{1,2,0:T(8,128)(2,1)}, u32[]{:S(2)}, u32[]{:S(2)}) collective-permute-start(bf16[4,128,1088]{1,2,0:T(8,128)(2,1)S(1)} %pad_maximum_fusion.12), channel_id=1, source_target_pairs={{7,0},{0,1},{1,2},{2,3},{3,4},{4,5},{5,6},{6,7},{15,8},{8,9},{9,10... | collective-permute-start | bytes 3342344 | tf_op jit(solution)/shard_map/while/body/eval_jaxpr/ppermute | solution.py:18
  660.3 16.9 %collective-permute-start = (bf16[4,128,1088]{1,2,0:T(8,128)(2,1)S(1)}, bf16[4,128,1088]{1,2,0:T(8,128)(2,1)}, u32[]{:S(2)}, u32[]{:S(2)}) collective-permute-start(bf16[4,128,1088]{1,2,0:T(8,128)(2,1)S(1)} %pad_maximum_fusion.12), channel_id=1, source_target_pairs={{7,0},{0,1},{1,2},{2,3},{3,4},{4,5},{5,6},{6,7},{15,8},{8,9},{9,10... | collective-permute-start | bytes 3342344 | tf_op jit(solution)/shard_map/while/body/eval_jaxpr/ppermute | solution.py:18
  683.9 16.9 %collective-permute-start = (bf16[4,128,1088]{1,2,0:T(8,128)(2,1)S(1)}, bf16[4,128,1088]{1,2,0:T(8,128)(2,1)}, u32[]{:S(2)}, u32[]{:S(2)}) collective-permute-start(bf16[4,128,1088]{1,2,0:T(8,128)(2,1)S(1)} %pad_maximum_fusion.12), channel_id=1, source_target_pairs={{7,0},{0,1},{1,2},{2,3},{3,4},{4,5},{5,6},{6,7},{15,8},{8,9},{9,10... | collective-permute-start | bytes 3342344 | tf_op jit(solution)/shard_map/while/body/eval_jaxpr/ppermute | solution.py:18
  707.5 16.9 %collective-permute-start = (bf16[4,128,1088]{1,2,0:T(8,128)(2,1)S(1)}, bf16[4,128,1088]{1,2,0:T(8,128)(2,1)}, u32[]{:S(2)}, u32[]{:S(2)}) collective-permute-start(bf16[4,128,1088]{1,2,0:T(8,128)(2,1)S(1)} %pad_maximum_fusion.12), channel_id=1, source_target_pairs={{7,0},{0,1},{1,2},{2,3},{3,4},{4,5},{5,6},{6,7},{15,8},{8,9},{9,10... | collective-permute-start | bytes 3342344 | tf_op jit(solution)/shard_map/while/body/eval_jaxpr/ppermute | solution.py:18
  731.0 16.9 %collective-permute-start = (bf16[4,128,1088]{1,2,0:T(8,128)(2,1)S(1)}, bf16[4,128,1088]{1,2,0:T(8,128)(2,1)}, u32[]{:S(2)}, u32[]{:S(2)}) collective-permute-start(bf16[4,128,1088]{1,2,0:T(8,128)(2,1)S(1)} %pad_maximum_fusion.12), channel_id=1, source_target_pairs={{7,0},{0,1},{1,2},{2,3},{3,4},{4,5},{5,6},{6,7},{15,8},{8,9},{9,10... | collective-permute-start | bytes 3342344 | tf_op jit(solution)/shard_map/while/body/eval_jaxpr/ppermute | solution.py:18
  754.6 16.9 %collective-permute-start = (bf16[4,128,1088]{1,2,0:T(8,128)(2,1)S(1)}, bf16[4,128,1088]{1,2,0:T(8,128)(2,1)}, u32[]{:S(2)}, u32[]{:S(2)}) collective-permute-start(bf16[4,128,1088]{1,2,0:T(8,128)(2,1)S(1)} %pad_maximum_fusion.12), channel_id=1, source_target_pairs={{7,0},{0,1},{1,2},{2,3},{3,4},{4,5},{5,6},{6,7},{15,8},{8,9},{9,10... | collective-permute-start | bytes 3342344 | tf_op jit(solution)/shard_map/while/body/eval_jaxpr/ppermute | solution.py:18
  803.7 307.5 %reduce-scatter.29.cloned.1.call-start = ((), (), s32[]{:S(2)}) async-start(), calls=%async_computation.24 | async-start | bytes 8460288
  810.5 36.2 %collective-permute-start.1 = (bf16[4,128,1088]{1,2,0:T(8,128)(2,1)S(1)}, bf16[4,128,1088]{1,2,0:T(8,128)(2,1)}, u32[]{:S(2)}, u32[]{:S(2)}) collective-permute-start(bf16[4,128,1088]{1,2,0:T(8,128)(2,1)S(1)} %pad_maximum_fusion.13), channel_id=1, source_target_pairs={{7,0},{0,1},{1,2},{2,3},{3,4},{4,5},{5,6},{6,7},{15,8},{8,9},{9,10... | collective-permute-start | bytes 3342344 | tf_op jit(solution)/shard_map/while/body/eval_jaxpr/ppermute | solution.py:18
  852.9 16.9 %collective-permute-start.1 = (bf16[4,128,1088]{1,2,0:T(8,128)(2,1)S(1)}, bf16[4,128,1088]{1,2,0:T(8,128)(2,1)}, u32[]{:S(2)}, u32[]{:S(2)}) collective-permute-start(bf16[4,128,1088]{1,2,0:T(8,128)(2,1)S(1)} %pad_maximum_fusion.13), channel_id=1, source_target_pairs={{7,0},{0,1},{1,2},{2,3},{3,4},{4,5},{5,6},{6,7},{15,8},{8,9},{9,10... | collective-permute-start | bytes 3342344 | tf_op jit(solution)/shard_map/while/body/eval_jaxpr/ppermute | solution.py:18
  876.0 16.9 %collective-permute-start.1 = (bf16[4,128,1088]{1,2,0:T(8,128)(2,1)S(1)}, bf16[4,128,1088]{1,2,0:T(8,128)(2,1)}, u32[]{:S(2)}, u32[]{:S(2)}) collective-permute-start(bf16[4,128,1088]{1,2,0:T(8,128)(2,1)S(1)} %pad_maximum_fusion.13), channel_id=1, source_target_pairs={{7,0},{0,1},{1,2},{2,3},{3,4},{4,5},{5,6},{6,7},{15,8},{8,9},{9,10... | collective-permute-start | bytes 3342344 | tf_op jit(solution)/shard_map/while/body/eval_jaxpr/ppermute | solution.py:18
  899.2 16.9 %collective-permute-start.1 = (bf16[4,128,1088]{1,2,0:T(8,128)(2,1)S(1)}, bf16[4,128,1088]{1,2,0:T(8,128)(2,1)}, u32[]{:S(2)}, u32[]{:S(2)}) collective-permute-start(bf16[4,128,1088]{1,2,0:T(8,128)(2,1)S(1)} %pad_maximum_fusion.13), channel_id=1, source_target_pairs={{7,0},{0,1},{1,2},{2,3},{3,4},{4,5},{5,6},{6,7},{15,8},{8,9},{9,10... | collective-permute-start | bytes 3342344 | tf_op jit(solution)/shard_map/while/body/eval_jaxpr/ppermute | solution.py:18
  922.3 16.9 %collective-permute-start.1 = (bf16[4,128,1088]{1,2,0:T(8,128)(2,1)S(1)}, bf16[4,128,1088]{1,2,0:T(8,128)(2,1)}, u32[]{:S(2)}, u32[]{:S(2)}) collective-permute-start(bf16[4,128,1088]{1,2,0:T(8,128)(2,1)S(1)} %pad_maximum_fusion.13), channel_id=1, source_target_pairs={{7,0},{0,1},{1,2},{2,3},{3,4},{4,5},{5,6},{6,7},{15,8},{8,9},{9,10... | collective-permute-start | bytes 3342344 | tf_op jit(solution)/shard_map/while/body/eval_jaxpr/ppermute | solution.py:18
  945.4 16.9 %collective-permute-start.1 = (bf16[4,128,1088]{1,2,0:T(8,128)(2,1)S(1)}, bf16[4,128,1088]{1,2,0:T(8,128)(2,1)}, u32[]{:S(2)}, u32[]{:S(2)}) collective-permute-start(bf16[4,128,1088]{1,2,0:T(8,128)(2,1)S(1)} %pad_maximum_fusion.13), channel_id=1, source_target_pairs={{7,0},{0,1},{1,2},{2,3},{3,4},{4,5},{5,6},{6,7},{15,8},{8,9},{9,10... | collective-permute-start | bytes 3342344 | tf_op jit(solution)/shard_map/while/body/eval_jaxpr/ppermute | solution.py:18
  1031.5 186.0 %reduce-scatter.19.cloned.1.call-start = ((), (), s32[]{:S(2)}) async-start(), calls=%async_computation.16 | async-start | bytes 11280384 | tf_op jit(solution)/shard_map/reduce_scatter | solution.py:360
  1054.6 263.6 %reduce-scatter.21.cloned.1.call-start = ((), (), s32[]{:S(2)}) async-start(), calls=%async_computation.17 | async-start | bytes 10653696 | tf_op jit(solution)/shard_map/reduce_scatter | solution.py:363
  1077.3 267.8 %reduce-scatter.25.cloned.1.call-start = ((), (), s32[]{:S(2)}) async-start(), calls=%async_computation.21 | async-start | bytes 696320
  1080.0 296.1 %reduce-scatter.23.cloned.1.call-start = ((), (), s32[]{:S(2)}) async-start(), calls=%async_computation.20 | async-start | bytes 1392640
  1113.5 321.5 %all-reduce.16.cloned.1.call-start = ((), (), s32[]{:S(2)}) async-start(), calls=%async_computation.23 | async-start | bytes 2506752
  1217.5 257.4 %reduce-scatter.27.cloned.1.call-start = ((), (), s32[]{:S(2)}) async-start(), calls=%async_computation.22 | async-start | bytes 2785280
  (197 other events, 1157.1 us)
Sparse Core Ops, SparseCore 0:
  9.7 32.8 all-gather.31
  49.9 77.6 all-gather.13
  129.2 41.9 all-gather.33
  172.7 31.8 all-gather.23
  206.0 30.8 all-gather.17
  238.4 30.7 all-gather.15
  270.8 30.7 all-gather.29
  303.2 30.7 all-gather.27
  336.5 37.6 all-gather.19
  375.9 96.6 all-gather.21
  474.4 101.2 all-gather.25
  803.8 42.2 reduce-scatter.30
  1031.6 79.4 reduce-scatter.28
  1113.4 104.0 reduce-scatter.18
  1219.7 98.4 reduce-scatter.20
  1321.8 23.3 reduce-scatter.24
  1347.9 28.1 reduce-scatter.22
  1379.1 55.7 all-reduce.15
  1438.2 36.5 reduce-scatter.26

commit v2 on v1

v2 whole, which is shorter than its diff:
```python
import jax
import jax.numpy as jnp
from jax import lax
from jax.sharding import PartitionSpec as P

HEADS = 17


EPS = 1e-05
GELU_C = 0.7978845608028654


def gelu_tanh(values):
    return 0.5 * values * (1.0 + jnp.tanh(GELU_C * (values + 0.044715 * values * values * values)))


def normalize(residual):
    row_mean = jnp.mean(residual, -1, keepdims=True)
    centered = residual - row_mean
    inv_std = lax.rsqrt(jnp.mean(centered * centered, -1, keepdims=True) + EPS)
    return (centered * inv_std, inv_std)


def norm_back(grad_normed, scaled, inv_std, gain_row):
    grad_scaled = grad_normed * gain_row
    return inv_std * (
        grad_scaled
        - jnp.mean(grad_scaled, -1, keepdims=True)
        - scaled * jnp.mean(grad_scaled * scaled, -1, keepdims=True)
    )


def running_total(counts):
    index = jnp.arange(counts.shape[0], dtype=jnp.int32)
    return jnp.sum(jnp.where(index[None, :] <= index[:, None], counts[None, :], 0), 1)


def segment_of(places, doc_ends):
    return jnp.sum((places[:, None] >= doc_ends[None, :]).astype(jnp.int32), 1)


def pair_swap(block):
    route = [(i, i ^ 1) for i in range(lax.axis_size("seq"))]
    return lax.ppermute(block, "seq", route)


def same_core():
    n_seq = lax.axis_size("seq")
    return [list(range(core, n_seq, 2)) for core in range(2)]


def gather_stack(shard):
    chips = lax.all_gather(shard, "seq", axis_index_groups=same_core())
    held = lax.all_gather(chips, "dp")
    other = pair_swap(held)
    first = lax.axis_index("seq") % 2 == 0
    both = jnp.stack([jnp.where(first, held, other), jnp.where(first, other, held)], 2)
    dp, chip_count = held.shape[:2]
    return both.transpose(1, 2, 0, 3, 4).reshape(2 * chip_count, dp, *shard.shape)


def pair_sum(parts):
    pairs = parts.reshape(parts.shape[0] // 2, 2, *parts.shape[1:])
    first = lax.axis_index("seq") % 2 == 0
    mine = jnp.where(first, pairs[:, 0], pairs[:, 1])
    other = jnp.where(first, pairs[:, 1], pairs[:, 0])
    got = pair_swap(other)
    return (mine.astype(jnp.float32) + got.astype(jnp.float32)).astype(jnp.bfloat16)


def scatter_stack(parts, after):
    held = pair_sum(parts).transpose(1, 0, 2, 3).reshape(-1, parts.shape[3])
    if after is not None:
        held, after = lax.optimization_barrier((held, after))
    held = lax.psum_scatter(held, "dp", scatter_dimension=0, tiled=True)
    held = lax.psum_scatter(
        held, "seq", scatter_dimension=0, axis_index_groups=same_core(), tiled=True
    )
    return held, after


def dot(left, right):
    return jnp.dot(left, right, preferred_element_type=jnp.float32)


def dot_right_t(left, right):
    return lax.dot_general(left, right, (((1,), (1,)), ((), ())), preferred_element_type=jnp.float32)


def dot_left_t(left, right):
    return lax.dot_general(left, right, (((0,), (0,)), ((), ())), preferred_element_type=jnp.float32)


def cols_of(rows, count):
    return rows.reshape(rows.shape[0], count, -1).transpose(1, 0, 2)


def apply_cols(rows, cols):
    lifted = jnp.broadcast_to(rows[None], (cols.shape[0],) + rows.shape)
    made = lax.dot_general(
        lifted, cols, (((2,), (1,)), ((0,), (0,))), preferred_element_type=jnp.float32
    )
    return made.transpose(1, 0, 2).reshape(rows.shape[0], -1)


def apply_cols_t(rows, cols):
    lifted = cols_of(rows, cols.shape[0])
    return lax.dot_general(
        lifted, cols, (((0, 2), (0, 2)), ((), ())), preferred_element_type=jnp.float32
    )


def grad_cols(left, right, count):
    lifted = jnp.broadcast_to(left[None], (count,) + left.shape)
    return lax.dot_general(
        lifted, cols_of(right, count), (((1,), (1,)), ((0,), (0,))),
        preferred_element_type=jnp.float32,
    )


def heads_of(rows, micro_count, head_dim):
    return rows.reshape(micro_count, -1, HEADS, head_dim).transpose(0, 2, 1, 3)


def rows_of(heads):
    micro_count, _, slots, head_dim = heads.shape
    return heads.transpose(0, 2, 1, 3).reshape(micro_count * slots, HEADS * head_dim)


def batched(left, right, left_dim, right_dim):
    return lax.dot_general(
        left,
        right,
        (((left_dim,), (right_dim,)), ((0, 1), (0, 1))),
        preferred_element_type=jnp.float32,
    )


def shards(
    tokens,
    cotangent,
    w_qkv,
    w_out,
    w_up,
    w_down,
    gain_one,
    bias_one,
    gain_two,
    bias_two,
    lengths,
    slot_order,
):
    micro_count, tok_dev, width = tokens.shape
    rows = micro_count * tok_dev
    head_dim = width // HEADS
    score_scale = head_dim ** (-0.5)
    n_seq = lax.axis_size("seq")
    my_slot = lax.axis_index("seq")
    bf16 = jnp.bfloat16

    norms = lax.all_gather(
        jnp.stack([gain_one, bias_one, gain_two, bias_two]), "dp", axis=1, tiled=True
    ).astype(jnp.float32)
    g_one, b_one, g_two, b_two = norms[0], norms[1], norms[2], norms[3]
    n_dp = lax.axis_size("dp")
    part, qkv_cols = w_qkv.shape
    out_cols = w_out.shape[1]
    up_cols = w_up.shape[1]
    fold = w_down.shape[0] // up_cols
    attn_stack = gather_stack(jnp.concatenate([w_qkv, w_out], 1))
    down_t = w_down.T
    ffn_stack = gather_stack(
        jnp.concatenate([w_up, *jnp.split(down_t, fold, 1)], 0)
    )
    cols_qkv = attn_stack[..., :qkv_cols].reshape(n_seq, width, qkv_cols)
    full_out = (
        attn_stack[..., qkv_cols:].reshape(n_seq, width, out_cols).transpose(1, 0, 2)
    ).reshape(width, width)
    cols_up = ffn_stack[:, :, :part].reshape(n_seq, width, up_cols)
    full_down_t = (
        ffn_stack[:, :, part:]
        .reshape(n_seq, n_dp, fold, out_cols, up_cols)
        .transpose(0, 3, 1, 2, 4)
        .reshape(width, fold * n_dp * up_cols)
    )

    doc_ends = jax.vmap(running_total)(lengths[:, 0])
    k_place = (
        slot_order[:, 0, :, None] * tok_dev + jnp.arange(tok_dev, dtype=jnp.int32)
    ).reshape(micro_count, n_seq * tok_dev)
    k_segment = jax.vmap(segment_of)(k_place, doc_ends)
    base_slot = lax.dynamic_slice_in_dim(slot_order[:, 0], my_slot, 1, 1)
    q_place = base_slot * tok_dev + jnp.arange(tok_dev, dtype=jnp.int32)
    q_segment = jax.vmap(segment_of)(q_place, doc_ends)
    allowed = (q_segment[:, :, None] == k_segment[:, None, :]) & (
        k_place[:, None, :] <= q_place[:, :, None]
    )

    residual = tokens.astype(jnp.float32).reshape(rows, width)
    scaled_one, inv_one = normalize(residual)
    normed_one = (scaled_one * g_one + b_one).astype(bf16)
    qkv_all = apply_cols(normed_one, cols_qkv).astype(bf16)
    queries = heads_of(qkv_all[:, :width], micro_count, head_dim)
    local_kv = qkv_all[:, width:].reshape(micro_count, tok_dev, 2 * width)
    group_kv = lax.all_gather(local_kv, "seq", axis=1, tiled=True)
    keys = heads_of(group_kv[..., :width], micro_count, head_dim)
    values = heads_of(group_kv[..., width:], micro_count, head_dim)

    scores = batched(queries, keys, 3, 3) * score_scale
    scores = jnp.where(allowed[:, None], scores, -jnp.inf)
    weights = jnp.exp(scores - jnp.max(scores, -1, keepdims=True))
    probs = weights * (1.0 / jnp.sum(weights, -1, keepdims=True))
    probs_low = probs.astype(bf16)
    attended = batched(probs_low, values, 3, 2)
    attn_flat = rows_of(attended.astype(bf16))
    middle = residual + dot(attn_flat, full_out)
    scaled_two, inv_two = normalize(middle)
    normed_two = (scaled_two * g_two + b_two).astype(bf16)
    hidden = apply_cols(normed_two, cols_up)
    activated_full, gelu_back = jax.vjp(gelu_tanh, hidden)
    activated = activated_full.astype(bf16)

    grad_rows = cotangent.reshape(rows, width)
    block_out = (middle + dot_right_t(activated, full_down_t)).astype(bf16)
    grad_hidden = gelu_back(dot(grad_rows, full_down_t))[0].astype(bf16)
    sum_down_t = dot_left_t(grad_rows, activated).astype(bf16)
    sum_down_t = (
        sum_down_t.reshape(n_seq, out_cols, n_dp, fold, up_cols)
        .transpose(0, 2, 3, 1, 4)
        .reshape(n_seq, n_dp, fold * out_cols, up_cols)
    )
    sum_up = grad_cols(normed_two, grad_hidden, n_seq).astype(bf16)
    sum_ffn, _ = scatter_stack(
        jnp.concatenate([sum_up.reshape(n_seq, n_dp, part, up_cols), sum_down_t], 2), None
    )
    grad_normed_two = apply_cols_t(grad_hidden, cols_up)
    grad_middle = grad_rows.astype(jnp.float32) + norm_back(
        grad_normed_two, scaled_two, inv_two, g_two
    )
    grad_branch = grad_middle.astype(bf16)
    sum_proj = grad_cols(attn_flat, grad_branch, n_seq).astype(bf16)
    grad_heads = heads_of(
        dot_right_t(grad_branch, full_out).astype(bf16), micro_count, head_dim
    )

    grad_probs = batched(grad_heads, values, 3, 3)
    row_dot = jnp.sum(probs * grad_probs, -1, keepdims=True)
    grad_scores = (probs * (grad_probs - row_dot)).astype(bf16)
    grad_query = rows_of(batched(grad_scores, keys, 3, 2) * score_scale)
    grad_keys = rows_of(batched(grad_scores, queries, 2, 2) * score_scale)
    grad_values = rows_of(batched(probs_low, grad_heads, 2, 2))
    grad_kv = jnp.concatenate([grad_keys.astype(bf16), grad_values.astype(bf16)], 1)
    grad_kv = grad_kv.reshape(micro_count, n_seq, tok_dev, 2 * width).transpose(1, 0, 2, 3)
    grad_kv = lax.psum_scatter(
        pair_sum(grad_kv), "seq", scatter_dimension=0, axis_index_groups=same_core()
    ).reshape(rows, 2 * width)
    grad_qkv_rows = jnp.concatenate([grad_query.astype(bf16), grad_kv], 1)
    sum_qkv = grad_cols(normed_one, grad_qkv_rows, n_seq).astype(bf16)
    sum_attn, sum_ffn = scatter_stack(
        jnp.concatenate([sum_qkv, sum_proj], 2).reshape(n_seq, n_dp, part, qkv_cols + out_cols),
        sum_ffn,
    )
    sum_attn = sum_attn.astype(jnp.float32)
    sum_ffn = sum_ffn.astype(jnp.float32)
    out_up = sum_ffn[:part]
    out_down = jnp.concatenate(jnp.split(sum_ffn[part:], fold, 0), 1).T
    out_qkv = sum_attn[:, :qkv_cols]
    out_proj = sum_attn[:, qkv_cols:]
    grad_normed_one = apply_cols_t(grad_qkv_rows, cols_qkv)
    grad_input = (
        grad_middle + norm_back(grad_normed_one, scaled_one, inv_one, g_one)
    ).astype(bf16)

    norm_sums = jnp.stack(
        [
            jnp.sum(grad_normed_one * scaled_one, 0),
            jnp.sum(grad_normed_one, 0),
            jnp.sum(grad_normed_two * scaled_two, 0),
            jnp.sum(grad_normed_two, 0),
        ]
    )
    norm_totals = lax.psum(norm_sums, ("dp", "seq"))
    norm_mine = lax.dynamic_slice_in_dim(norm_totals, lax.axis_index("dp") * part, part, 1)
    return (
        block_out.reshape(tokens.shape),
        grad_input.reshape(tokens.shape),
        out_qkv,
        out_proj,
        out_up,
        out_down,
        norm_mine[0],
        norm_mine[1],
        norm_mine[2],
        norm_mine[3],
    )


def solution(mesh):
    return jax.shard_map(
        shards,
        mesh=mesh,
        in_specs=(
            P(None, ("dp", "seq"), None),
            P(None, ("dp", "seq"), None),
            P("dp", "seq"),
            P("dp", "seq"),
            P("dp", "seq"),
            P("dp", "seq"),
            P("dp"),
            P("dp"),
            P("dp"),
            P("dp"),
            P(None, "dp", None),
            P(None, "dp", None),
        ),
        out_specs=(
            P(None, ("dp", "seq"), None),
            P(None, ("dp", "seq"), None),
            P("dp", "seq"),
            P("dp", "seq"),
            P("dp", "seq"),
            P("dp", "seq"),
            P("dp"),
            P("dp"),
            P("dp"),
            P("dp"),
        ),
        check_vma=False,
    )
```

time: 1490 us -> 1000 us (0.67)
  waiting for transfers between devices: 1000 us -> 451 us
  local copies, waits for them, and re-layouts: 127 us -> 225 us
  matrix products: 202 us -> 117 us
  other arithmetic: 58.9 us -> 132 us
  blocking collectives: 68.8 us -> 49.2 us
    ppermute x16 -> x5, waiting for transfers between devices: 257 us -> 14.4 us  [pair_swap(): return lax.ppermute(block, 'seq', route)]
    all_gather x11 -> x5, waiting for transfers between devices: 421 us -> 221 us  [the longest x2 129 us: gather_stack(): held = lax.all_gather(chips, 'dp')]
    dot_general x112 -> x17, matrix products: 202 us -> 105 us  [the longest x5 40 us: batched(): lax.dot_general(left, right, (((left_dim,), (right_dim,)), ((0, 1), (0, 1...]
    reduce_scatter x2 -> x3, waiting for transfers between devices: 159 us -> 94.3 us  [the longest x1 56.6 us: scatter_stack(): held = lax.psum_scatter(held, 'dp', scatter_dimension=0, tiled=True)]
    reshape x4 -> x8, local copies, waits for them, and re-layouts: 12.6 us -> 75.7 us  [the longest x2 41.4 us: shards(): sum_down_t.reshape(n_seq, out_cols, n_dp, fold, up_cols)]
    unnamed x25 -> x12, waiting for transfers between devices: 164 us -> 121 us
    transpose x4 -> x5, other arithmetic: 0.05 us -> 40.8 us  [the longest x2 23.4 us: scatter_stack(): held = pair_sum(parts).transpose(1, 0, 2, 3).reshape(-1, parts.shape[3])]
    transpose x0 -> x4, local copies, waits for them, and re-layouts: none -> 40 us  [the longest x2 17.6 us: gather_stack(): both.transpose(1, 2, 0, 3, 4).reshape(2 * chip_count, dp, *shard.shape)]
  transfers between devices with their start and end apart: 35 -> 15, of which waited for: 34 -> 11; matrix products, arithmetic and copies ran while one was open for 16% -> 33% of each run, Pallas kernels for 0% -> 0%
where the time goes in v2:
time: 1000 us; the launch traced here: 990 us
  waiting for transfers between devices  451 us (45%)
  local copies, waits for them, and re-layouts  225 us (22%)
  other arithmetic  132 us (13%)
  matrix products  117 us (12%)
  blocking collectives  49.2 us (5%)
  between operations  15.5 us (2%)
    all_gather x2, waiting for transfers between devices, gather_stack(): held = lax.all_gather(chips, 'dp')  129 us
    unnamed x12, waiting for transfers between devices  121 us
    all_gather x2, waiting for transfers between devices, gather_stack(): chips = lax.all_gather(shard, 'seq', axis_index_groups=same_core())  92.4 us
    reduce_scatter x1, waiting for transfers between devices, scatter_stack(): held = lax.psum_scatter(held, 'dp', scatter_dimension=0, tiled=True)  56.6 us
    reshape x2, local copies, waits for them, and re-layouts, shards(): sum_down_t.reshape(n_seq, out_cols, n_dp, fold, up_cols)  41.4 us
    psum x1, blocking collectives, shards(): norm_totals = lax.psum(norm_sums, ('dp', 'seq'))  41.1 us
    dot_general x5, matrix products, batched(): lax.dot_general(left, right, (((left_dim,), (right_dim,)), ((0, 1), (0, 1...  40 us
    reduce_scatter x1, waiting for transfers between devices, shards(): lax.psum_scatter(pair_sum(grad_kv), 'seq', scatter_dimension=0, axis_inde...  37.7 us
  transfers between devices with their start and end apart: 15, of which 11 were waited for; matrix products, arithmetic and copies ran while one was open for 33% of the time, Pallas kernels for 0%

profile of v2, /device:TPU:0, one launch (start us, length us, event | category | flops | bytes accessed | tf_op | source)
XLA Modules:
  0.0 990.3 jit_solution(6537300546122881620)
XLA Ops:
  13.4 33.8 %all-gather.13.cloned.1.call-done = bf16[1088,544]{1,0:T(8,128)(2,1)} async-done(((bf16[272,544]{1,0:T(8,128)(2,1)}), bf16[1088,544]{1,0:T(8,128)(2,1)}) %all-gather.13.cloned.1.call-update) | async-done | bytes 1183760 | tf_op jit(solution)/shard_map/all_gather | solution.py:53
  47.3 58.6 %all-gather.17.cloned.1.call-done = bf16[2176,544]{1,0:T(8,128)(2,1)} async-done(((bf16[544,544]{1,0:T(8,128)(2,1)}), bf16[2176,544]{1,0:T(8,128)(2,1)}) %all-gather.17.cloned.1.call-update) | async-done | bytes 2367504 | tf_op jit(solution)/shard_map/all_gather | solution.py:53
  105.9 64.7 %all-gather.15.cloned.1.call-done = bf16[16,272,544]{2,1,0:T(8,128)(2,1)} async-done(((bf16[4,272,544]{2,1,0:T(8,128)(2,1)}), bf16[16,272,544]{2,1,0:T(8,128)(2,1)}) %all-gather.15.cloned.1.call-update) | async-done | bytes 4734992 | tf_op jit(solution)/shard_map/all_gather | solution.py:54
  180.0 11.1 %select_bitcast_fusion.3 = (bf16[4,4,1,272,544]{4,3,1,0,2:T(8,128)(2,1)}, bf16[4,4,1,272,544]{4,3,1,0,2:T(8,128)(2,1)}) fusion(bf16[4,4,272,544]{3,2,1,0:T(8,128)(2,1)} %bitcast.351, bf16[4,4,272,544]{3,2,1,0:T(8,128)(2,1)} %collective-permute-done, pred[]{:T(512)S(6)} %eq.33), kind=kLoop, calls=%fused_computation.48 | loop fusion | flops 4734976 | bytes 18939904 | tf_op jit(solution)/shard_map/stack | solution.py:57
  218.9 63.9 %all-gather.19.cloned.1.call-done = bf16[16,544,544]{2,1,0:T(8,128)(2,1)} async-done(((bf16[4,544,544]{2,1,0:T(8,128)(2,1)}), bf16[16,544,544]{2,1,0:T(8,128)(2,1)}) %all-gather.19.cloned.1.call-update) | async-done | bytes 9469968 | tf_op jit(solution)/shard_map/all_gather | solution.py:54
  300.3 9.0 select_bitcast_fusion.1
  309.3 10.5 %maximum_bitcast_fusion = bf16[4,2,4,544,544]{4,3,0,2,1:T(8,128)(2,1)} fusion(bf16[4,4,1,544,544]{4,3,1,0,2:T(8,128)(2,1)S(1)} %get-tuple-element.93, bf16[4,4,1,544,544]{4,3,1,0,2:T(8,128)(2,1)S(1)} %get-tuple-element.92), kind=kLoop, calls=%fused_computation.1 | loop fusion | flops 9469952 | bytes 37879808 | tf_op jit(solution)/shard_map/transpose | solution.py:59
  319.8 11.9 %copy.216 = bf16[4,2,4,544,544]{4,3,2,1,0:T(8,128)(2,1)S(1)} copy(bf16[4,2,4,544,544]{4,3,0,2,1:T(8,128)(2,1)} %maximum_bitcast_fusion) | data formatting | bytes 37879808 | tf_op jit(solution)/shard_map/transpose | solution.py:59
  331.8 9.0 fusion.82
  340.8 16.9 %copy.218 = bf16[8,136,4,2,544]{4,3,2,1,0:T(2,128)(2,1)} copy(bf16[8,136,4,2,544]{4,1,3,2,0:T(8,128)(2,1)} %bitcast.326) | data formatting | bytes 18939904 | tf_op jit(solution)/shard_map/transpose | solution.py:183
  357.7 23.4 %reshape.359 = bf16[1088,4352]{1,0:T(8,128)(2,1)} reshape(bf16[8,136,4,2,544]{4,3,2,1,0:T(2,128)(2,1)} %copy.218) | data formatting | bytes 18939904 | tf_op jit(solution)/shard_map/reshape | solution.py:184
  389.2 11.8 %fusion.86 = (f32[2,17,128]{2,1,0:T(8,128)S(1)}, f32[2,17,128,1024]{3,2,1,0:T(8,128)}) fusion(pred[2,128,1024]{2,1,0:T(8,128)(4,1)S(1)} %copy-done.20, bf16[2,17,1024,64]{2,3,1,0:T(8,128)(2,1)} %bitcast.337, bf16[2,128,17,64]{1,0,3,2:T(2,128)(2,1)S(1)} %reshape.349), kind=kOutput, calls=%fused_computation.178 | convolution fusion | flops 588252160 | bytes 23118848 | tf_op jit(solution)/shard_map/sub | solution.py:211
  401.1 9.4 fusion.49
  412.6 11.4 %fusion.24 = (bf16[256,8,544]{0,2,1:T(8,128)(2,1)}, f32[8,256,544]{1,2,0:T(8,128)}) fusion(bf16[8,1088,544]{2,1,0:T(8,128)(2,1)} %bitcast.342, bf16[256,1088]{0,1:T(8,128)(2,1)S(1)} %add_convert_fusion.1), kind=kOutput, calls=%fused_computation.57 | convolution fusion | flops 2434334720 | bytes 16711680 | tf_op jit(solution)/shard_map/dot_general | solution.py:100
  427.6 9.4 fusion.19
  446.1 10.0 %fusion.33 = bf16[2,17,1024,64]{2,3,1,0:T(8,128)(2,1)} fusion(f32[2,17,128,1024]{3,2,1,0:T(8,128)} %get-tuple-element.105, f32[2,17,128]{2,1,0:T(8,128)S(1)} %broadcast_divide_fusion, bf16[2,128,17,64]{1,0,3,2:T(2,128)(2,1)S(1)} %reshape.364), kind=kOutput, calls=%fused_computation.74 | convolution fusion | flops 581566464 | bytes 22856704 | tf_op jit(solution)/shard_map/dot_general | solution.py:131
  456.1 11.2 %multiply_reduce_fusion = (f32[2,17,128]{2,1,0:T(8,128)S(1)}, f32[2,17,128,1024]{3,2,1,0:T(8,128)}) fusion(f32[2,17,128,1024]{3,2,1,0:T(8,128)} %get-tuple-element.105, f32[2,17,128]{2,1,0:T(8,128)S(1)} %broadcast_divide_fusion, bf16[2,17,1024,64]{2,3,1,0:T(8,128)(2,1)S(1)} %bitcast.331, bf16[2,128,17,64]{1,0,3,2:T(2,128)(2,1)S(1)} %reshape.364), kind=kOutput, calls=%fused_computation.9 | convolution fusion | flops 583790336 | bytes 40699904 | tf_op jit(solution)/shard_map/dot_general | solution.py:131
  479.5 12.1 %multiply_convert_fusion = bf16[2,17,128,1024]{3,2,1,0:T(8,128)(2,1)S(1)} fusion(f32[2,17,128,1024]{3,2,1,0:T(8,128)} %get-tuple-element.112, f32[2,17,128,1024]{3,2,1,0:T(8,128)} %get-tuple-element.105, f32[2,17,128]{2,1,0:T(8,128)S(1)} %get-tuple-element.111, f32[2,17,128]{2,1,0:T(8,128)S(1)} %broadcast_divide_fusion), kind=kLoop, calls=%fused_computation.8 | loop fusion | flops 17825792 | bytes 44599296 | tf_op jit(solution)/shard_map/convert_element_type | solution.py:248
  522.1 29.8 %reshape.370 = bf16[8,136,4,2,544]{4,3,2,1,0:T(2,128)(2,1)} reshape(bf16[1088,4352]{1,0:T(8,128)(2,1)} %fusion.2) | data formatting | bytes 18939904 | tf_op jit(solution)/shard_map/reshape | solution.py:228
  552.0 11.5 %copy.234 = bf16[8,136,4,2,544]{4,1,3,2,0:T(8,128)(2,1)} copy(bf16[8,136,4,2,544]{4,3,2,1,0:T(2,128)(2,1)} %reshape.370) | data formatting | bytes 18939904 | tf_op jit(solution)/shard_map/reshape | solution.py:228
  569.1 14.3 %copy.233 = bf16[8,1088,544]{2,1,0:T(8,128)(2,1)} copy(bf16[8,1088,544]{1,2,0:T(8,128)(2,1)} %convolution_convert_fusion.2) | data formatting | bytes 18939904 | tf_op jit(solution)/shard_map/convert_element_type | solution.py:232
  583.4 16.0 %fusion.4 = bf16[4,4,544,544]{3,2,1,0:T(8,128)(2,1)} fusion(pred[]{:T(512)S(6)} %eq.33, bf16[4,2,4,272,544]{4,3,2,1,0:T(8,128)(2,1)} %bitcast.317, bf16[4,2,4,272,544]{4,3,2,1,0:T(8,128)(2,1)} %bitcast.313), kind=kLoop, calls=%fused_computation.17 | loop fusion | flops 42614784 | bytes 28409856 | tf_op jit(solution)/shard_map/jit(_where)/select_n | solution.py:66
  604.7 12.2 %collective-permute-done.4 = bf16[4,4,544,544]{3,2,1,0:T(8,128)(2,1)} collective-permute-done((bf16[4,4,544,544]{3,2,1,0:T(8,128)(2,1)}, bf16[4,4,544,544]{3,2,1,0:T(8,128)(2,1)}, u32[]{:S(2)}, u32[]{:S(2)}) %collective-permute-start.4) | collective-permute-done | bytes 9469984 | tf_op jit(solution)/shard_map/ppermute | solution.py:44
  616.9 12.9 %fusion.5 = bf16[4,4,544,544]{3,2,0,1:T(8,128)(2,1)S(1)} fusion(bf16[4,4,544,544]{3,2,1,0:T(8,128)(2,1)} %collective-permute-done.4, pred[]{:T(512)S(6)} %eq.33, bf16[4,2,4,272,544]{4,3,2,1,0:T(8,128)(2,1)} %bitcast.318, bf16[4,2,4,272,544]{4,3,2,1,0:T(8,128)(2,1)} %bitcast.314), kind=kLoop, calls=%fused_computation.18 | loop fusion | flops 61554688 | bytes 37879808 | tf_op jit(solution)/shard_map/transpose | solution.py:72
  648.3 37.7 %reduce-scatter.10.cloned.1.call-done = bf16[1,2,128,2176]{3,2,1,0:T(8,128)(2,1)} async-done(((bf16[4,2,128,2176]{3,2,1,0:T(8,128)(2,1)}), bf16[1,2,128,2176]{3,2,1,0:T(8,128)(2,1)}) %reduce-scatter.10.cloned.1.call-update) | async-done | bytes 1114128 | tf_op jit(solution)/shard_map/reduce_scatter | solution.py:254
  696.7 14.5 %copy.227 = bf16[8,1088,544]{2,1,0:T(8,128)(2,1)} copy(bf16[8,1088,544]{1,2,0:T(8,128)(2,1)} %pad_maximum_fusion.1) | data formatting | bytes 18939904 | tf_op jit(solution)/shard_map/concatenate | solution.py:260
  718.7 79.8 %reduce-scatter.16.cloned.1.call-done = bf16[2176,544]{1,0:T(8,128)(2,1)} async-done(((bf16[8704,544]{1,0:T(8,128)(2,1)}), bf16[2176,544]{1,0:T(8,128)(2,1)}) %reduce-scatter.16.cloned.1.call-update) | async-done | bytes 2367504
  798.6 10.5 %fusion.14 = bf16[4,4,272,544]{3,2,0,1:T(8,128)(2,1)} fusion(bf16[4,4,272,544]{3,2,1,0:T(8,128)(2,1)} %collective-permute-done.3, pred[]{:T(512)S(6)} %eq.33, bf16[4,2,4,272,544]{4,3,2,1,0:T(8,128)(2,1)} %bitcast.316), kind=kLoop, calls=%fused_computation.44 | loop fusion | flops 11837440 | bytes 18939904 | tf_op jit(solution)/shard_map/transpose | solution.py:72
  814.6 41.0 %reduce-scatter.18.cloned.1.call-done = bf16[544,544]{1,0:T(8,128)(2,1)} async-done(((bf16[2176,544]{1,0:T(8,128)(2,1)}), bf16[544,544]{1,0:T(8,128)(2,1)}) %reduce-scatter.18.cloned.1.call-update) | async-done | bytes 591888
  866.3 56.6 %reduce-scatter.12.cloned.1.call-done = bf16[1088,544]{1,0:T(8,128)(2,1)} async-done(((bf16[4352,544]{1,0:T(8,128)(2,1)}), bf16[1088,544]{1,0:T(8,128)(2,1)}) %reduce-scatter.12.cloned.1.call-update) | async-done | bytes 1183760 | tf_op jit(solution)/shard_map/reduce_scatter | solution.py:75
  923.0 8.4 multiply_reduce_fusion.2
  931.4 41.1 %psum.7 = f32[4,1088]{1,0:T(4,128)S(1)} all-reduce(f32[4,1088]{1,0:T(4,128)S(1)} %pad_maximum_fusion.6), channel_id=1, replica_groups=mesh['dp'=4,'seq'=8] {'dp','seq'}, use_global_device_ids=true, to_apply=%region_23.24 | all-reduce | flops 4352 | bytes 34816 | tf_op jit(solution)/shard_map/psum | solution.py:282
  (235 shorter events, 200.2 us)
Async XLA Ops:
  7.2 420.1 %copy-start = (bf16[2,128,1088]{1,2,0:T(8,128)(2,1)S(1)}, bf16[2,128,1088]{1,2,0:T(8,128)(2,1)}, u32[]{:S(2)}) copy-start(bf16[2,128,1088]{1,2,0:T(8,128)(2,1)} %param.13) | copy-start | bytes 1671172
  7.2 163.4 %copy-start.41 = (bf16[272]{0:T(512)(128)(2,1)S(1)}, bf16[272]{0:T(512)(128)(2,1)}, u32[]{:S(2)}) copy-start(bf16[272]{0:T(512)(128)(2,1)} %param.21) | copy-start | bytes 1636
  7.2 163.4 %copy-start.42 = (bf16[272]{0:T(512)(128)(2,1)S(1)}, bf16[272]{0:T(512)(128)(2,1)}, u32[]{:S(2)}) copy-start(bf16[272]{0:T(512)(128)(2,1)} %param.20) | copy-start | bytes 1636
  7.2 163.4 %copy-start.43 = (bf16[272]{0:T(512)(128)(2,1)S(1)}, bf16[272]{0:T(512)(128)(2,1)}, u32[]{:S(2)}) copy-start(bf16[272]{0:T(512)(128)(2,1)} %param.19) | copy-start | bytes 1636
  7.2 163.4 %copy-start.44 = (bf16[272]{0:T(512)(128)(2,1)S(1)}, bf16[272]{0:T(512)(128)(2,1)}, u32[]{:S(2)}) copy-start(bf16[272]{0:T(512)(128)(2,1)} %param.18) | copy-start | bytes 1636
  7.2 171.7 %copy-start.5 = (bf16[2,128,1088]{1,2,0:T(8,128)(2,1)S(1)}, bf16[2,128,1088]{1,2,0:T(8,128)(2,1)}, u32[]{:S(2)}) copy-start(bf16[2,128,1088]{1,2,0:T(8,128)(2,1)} %param.12) | copy-start | bytes 1671172
  7.2 39.9 %all-gather.13.cloned.1.call-start = ((), (), s32[]{:S(2)}) async-start(), calls=%async_computation.9 | async-start | bytes 1740800 | tf_op jit(solution)/shard_map/all_gather | solution.py:53
  10.2 95.6 %all-gather.17.cloned.1.call-start = ((), (), s32[]{:S(2)}) async-start(), calls=%async_computation.11 | async-start | bytes 3481600 | tf_op jit(solution)/shard_map/all_gather | solution.py:53
  13.3 157.3 %all-gather.15.cloned.1.call-start = ((), (), s32[]{:S(2)}) async-start(), calls=%async_computation.10 | async-start | bytes 6963200 | tf_op jit(solution)/shard_map/all_gather | solution.py:54
  47.2 235.6 %all-gather.19.cloned.1.call-start = ((), (), s32[]{:S(2)}) async-start(), calls=%async_computation.12 | async-start | bytes 13926400 | tf_op jit(solution)/shard_map/all_gather | solution.py:54
  105.8 275.3 %all-gather.11.cloned.1.call-start = ((), (), s32[]{:S(2)}) async-start(), calls=%async_computation.5 | async-start | bytes 10027008 | tf_op jit(solution)/shard_map/all_gather | solution.py:205
  170.6 9.5 collective-permute-start
  179.0 262.0 %copy-start.21 = (f32[1088]{0:T(1024)}, f32[1088]{0:T(1024)S(1)}, u32[]{:S(2)}) copy-start(f32[1088]{0:T(1024)S(1)} %get-tuple-element.86) | copy-start | bytes 13060
  211.3 71.5 %copy-start.39 = (s32[2,1,8]{2,1,0:T(1,128)S(1)}, s32[2,1,8]{2,1,0:T(1,128)}, u32[]{:S(2)}) copy-start(s32[2,1,8]{2,1,0:T(1,128)} %param.23) | copy-start | bytes 196
  211.3 71.7 %copy-start.40 = (s32[2,1,8]{2,1,0:T(1,128)S(1)}, s32[2,1,8]{2,1,0:T(1,128)}, u32[]{:S(2)}) copy-start(s32[2,1,8]{2,1,0:T(1,128)} %param.22) | copy-start | bytes 196
  218.8 467.1 %reduce-scatter.10.cloned.1.call-start = ((), (), s32[]{:S(2)}) async-start(), calls=%async_computation.6 | async-start | bytes 5570560 | tf_op jit(solution)/shard_map/reduce_scatter | solution.py:254
  282.8 17.4 %collective-permute-start.1 = (bf16[4,4,544,544]{3,2,1,0:T(8,128)(2,1)}, bf16[4,4,544,544]{3,2,1,0:T(8,128)(2,1)}, u32[]{:S(2)}, u32[]{:S(2)}) collective-permute-start(bf16[4,4,544,544]{3,2,1,0:T(8,128)(2,1)} %bitcast.340), channel_id=1, source_target_pairs={{0,1},{1,0},{2,3},{3,2},{4,5},{5,4},{6,7},{7,6},{8,9},{9,8},{10,11... | collective-permute-start | bytes 28409864 | tf_op jit(solution)/shard_map/ppermute | solution.py:44
  516.9 83.0 %collective-permute-start.2 = (bf16[4,2,128,2176]{3,2,1,0:T(8,128)(2,1)}, bf16[4,2,128,2176]{3,2,1,0:T(8,128)(2,1)}, u32[]{:S(2)}, u32[]{:S(2)}) collective-permute-start(bf16[4,2,128,2176]{3,2,1,0:T(8,128)(2,1)} %select_bitcast_fusion.4), channel_id=1, source_target_pairs={{0,1},{1,0},{2,3},{3,2},{4,5},{5,4},{6,7},{7,6},{8,9},{9,8},{10,11... | collective-permute-start | bytes 13369352 | tf_op jit(solution)/shard_map/ppermute | solution.py:44
  599.5 17.4 %collective-permute-start.4 = (bf16[4,4,544,544]{3,2,1,0:T(8,128)(2,1)}, bf16[4,4,544,544]{3,2,1,0:T(8,128)(2,1)}, u32[]{:S(2)}, u32[]{:S(2)}) collective-permute-start(bf16[4,4,544,544]{3,2,1,0:T(8,128)(2,1)} %fusion.4), channel_id=1, source_target_pairs={{0,1},{1,0},{2,3},{3,2},{4,5},{5,4},{6,7},{7,6},{8,9},{9,8},{10,11... | collective-permute-start | bytes 28409864 | tf_op jit(solution)/shard_map/ppermute | solution.py:44
  604.6 193.9 %reduce-scatter.16.cloned.1.call-start = ((), (), s32[]{:S(2)}) async-start(), calls=%async_computation.13 | async-start | bytes 13926400
  635.5 220.0 %reduce-scatter.18.cloned.1.call-start = ((), (), s32[]{:S(2)}) async-start(), calls=%async_computation.14 | async-start | bytes 3481600
  718.7 79.9 %collective-permute-start.3 = (bf16[4,4,272,544]{3,2,1,0:T(8,128)(2,1)}, bf16[4,4,272,544]{3,2,1,0:T(8,128)(2,1)}, u32[]{:S(2)}, u32[]{:S(2)}) collective-permute-start(bf16[4,4,272,544]{3,2,1,0:T(8,128)(2,1)} %fusion.13), channel_id=1, source_target_pairs={{0,1},{1,0},{2,3},{3,2},{4,5},{5,4},{6,7},{7,6},{8,9},{9,8},{10,11... | collective-permute-start | bytes 14204936 | tf_op jit(solution)/shard_map/ppermute | solution.py:44
  798.6 124.3 %reduce-scatter.12.cloned.1.call-start = ((), (), s32[]{:S(2)}) async-start(), calls=%async_computation.7 | async-start | bytes 6963200 | tf_op jit(solution)/shard_map/reduce_scatter | solution.py:75
  857.0 122.3 %reduce-scatter.14.cloned.1.call-start = ((), (), s32[]{:S(2)}) async-start(), calls=%async_computation.8 | async-start | bytes 1740800 | tf_op jit(solution)/shard_map/reduce_scatter | solution.py:76
  858.4 64.5 %copy-start.24 = (f32[1088]{0:T(1024)S(1)}, f32[1088]{0:T(1024)}, u32[]{:S(2)}) copy-start(f32[1088]{0:T(1024)} %copy-done.23) | copy-start | bytes 13060
  858.4 64.5 %copy-start.34 = (f32[256]{0:T(256)S(1)}, f32[256]{0:T(256)}, u32[]{:S(2)}) copy-start(f32[256]{0:T(256)} %copy-done.33) | copy-start | bytes 3076
  858.4 64.5 %copy-start.36 = (f32[256]{0:T(256)S(1)}, f32[256]{0:T(256)}, u32[]{:S(2)}) copy-start(f32[256]{0:T(256)} %copy-done.35) | copy-start | bytes 3076
  923.0 50.2 %copy-start.22 = (f32[1088]{0:T(1024)S(1)}, f32[1088]{0:T(1024)}, u32[]{:S(2)}) copy-start(f32[1088]{0:T(1024)} %copy-done.21) | copy-start | bytes 13060
  923.0 50.2 %copy-start.26 = (f32[256]{0:T(256)S(1)}, f32[256]{0:T(256)}, u32[]{:S(2)}) copy-start(f32[256]{0:T(256)} %copy-done.25) | copy-start | bytes 3076
  923.0 50.2 %copy-start.28 = (f32[256]{0:T(256)S(1)}, f32[256]{0:T(256)}, u32[]{:S(2)}) copy-start(f32[256]{0:T(256)} %copy-done.27) | copy-start | bytes 3076
  923.0 50.2 %copy-start.30 = (f32[256]{0:T(256)S(1)}, f32[256]{0:T(256)}, u32[]{:S(2)}) copy-start(f32[256]{0:T(256)} %copy-done.29) | copy-start | bytes 3076
  923.0 50.2 %copy-start.32 = (f32[256]{0:T(256)S(1)}, f32[256]{0:T(256)}, u32[]{:S(2)}) copy-start(f32[256]{0:T(256)} %copy-done.31) | copy-start | bytes 3076
  (36 other events, 478.5 us)
Sparse Core Ops, SparseCore 0:
  10.3 36.7 all-gather.12
  49.3 56.4 all-gather.16
  107.7 62.8 all-gather.14
  172.3 110.5 all-gather.18
  284.3 86.8 all-gather.10
  604.8 81.1 reduce-scatter.9
  689.1 109.3 reduce-scatter.15
  800.9 54.6 reduce-scatter.17
  858.9 63.9 reduce-scatter.11
  925.2 33.3 reduce-scatter.13
